TPU v7x, 128 devices: a whole 4x4x4 slice. The times are simulated.
128 devices in a mesh: lon: 16 (over y_lo, z, core), filt: 8 (over y_hi, x).
Axes of the slice: x: 4, y: 4 (y_hi: 2, y_lo: 2; y = y_hi * 2 + y_lo), z: 4, core: 2. Of those that a mesh axis runs over, the one named last changes fastest.
Arguments:
- ocean_state: bfloat16 [256, 16, 4096], P(None, None, 'lon'), may hold values from -6 to 6
- cotangent: bfloat16 [256, 16, 4096], P(None, None, 'lon'), may hold values from -6 to 6
- conv_in: bfloat16 [9, 256, 1024], P(None, None, 'filt'), may hold values from -0.1875 to 0.1875
- conv_out: bfloat16 [9, 1024, 256], P(None, 'filt'), may hold values from -0.09375 to 0.09375
- tile_mask: int32 [2, 32], replicated, may hold values from 0 to 1, as said below
Outputs:
- block_out: bfloat16 [256, 16, 4096], P('filt', None, 'lon')
- grad_state: bfloat16 [256, 16, 4096], P('filt', None, 'lon')
- grad_conv_in: float32 [9, 256, 1024], P(None, None, 'filt')
- grad_conv_out: float32 [9, 1024, 256], P(None, 'filt')
Inputs may be any that keep to these rules, and one draw needn't show every extreme that they name: `tile_mask`: 1 marks an ocean tile of 8 x 128 cells, 0 a land tile; every tile of the first tile row is ocean, and the last tile row holds land.
All inputs are finite; a program needn't handle non-finite values.
Results may differ from a plain program's by a relative error of at most 0.0037.
Values may be sent and summed in bfloat16 or wider, within the bound.
A program may use at most 192 MiB of HBM per device.

v0:
```python
import functools

import jax
import jax.numpy as jnp
from jax import lax
from jax.experimental import pallas as pl
from jax.experimental.pallas import tpu as pltpu
from jax.sharding import PartitionSpec as P

TILE_H = 8
TILE_W = 128
MESH = pl.DeviceIdType.MESH
BF = jnp.bfloat16
F32 = jnp.float32
ROOT_HALF = 0.7071067811865476
NORM_CONST = 0.3989422804014327


def dot(a, b):
    return lax.dot_general(a, b, (((1,), (0,)), ((), ())), preferred_element_type=F32)


def dot_t(a, b):
    return lax.dot_general(a, b, (((1,), (1,)), ((), ())), preferred_element_type=F32)


def gelu_parts(v):
    e = 0.5 * (1.0 + lax.erf(v * ROOT_HALF))
    return v * e, e + v * jnp.exp(-0.5 * v * v) * NORM_CONST


def coords():
    lon, filt = lax.axis_index("lon"), lax.axis_index("filt")
    y, x = filt // 4, filt % 4
    v = x // 2
    u = (x + v) % 2
    return lon, filt, u, v, y


def filt_of(u, v, y):
    return 4 * y + 2 * v + (u + v) % 2


def kernel(
    x_ref, c_ref, xh_ref, ch_ref, w1_ref, w2_ref, w3_ref, w4_ref, mask_ref, maskh_ref,
    sums_ref, grads_ref,
    hs, gps, edge, hedge, keep, s1, r1, s2, r2, s3, r3,
    gacc, gx, gxr, gsum, gs, gr, gall, goth,
    send_sem, recv_sem, gxs_sem, gxr_sem, gs_sem, gr_sem, ga_sem, gar_sem, go_sem, gor_sem, out_sem,
):
    lon, filt, u, v, y = coords()
    core = lon % 2
    chip = lon // 2
    lane256 = lax.broadcasted_iota(jnp.int32, (128, 256), 1)
    partners = ((lon, filt_of(1 - u, v, y)), (lon, filt_of(u, 1 - v, y)), (lon, filt_of(u, v, 1 - y)))
    mate = (chip * 2 + (1 - core), filt)

    def peer(d):
        z, yl = chip % 4, chip // 4
        z = (z + d % 4) % 4
        yl = (yl + d // 4) % 2
        return yl * 4 + z

    def opposite(d):
        return (4 - d % 4) % 4 + (d // 4) * 4

    barrier = pltpu.get_barrier_semaphore()
    for who in partners + (mate,):
        pl.semaphore_signal(barrier, inc=1, device_id=who, device_id_type=MESH)
    for d in range(1, 8):
        pl.semaphore_signal(barrier, inc=1, device_id=(peer(d) * 2 + core, filt), device_id_type=MESH)

    lane_h = lax.broadcasted_iota(jnp.int32, (384, 128), 1) % 16

    def halo(w_ref, t_ref):
        total = dot(w_ref[:, 256:512], t_ref[...])
        above = pltpu.roll(dot(w_ref[:, 0:256], t_ref[...]), 1, 1)
        below = pltpu.roll(dot(w_ref[:, 512:768], t_ref[...]), 127, 1)
        return total + jnp.where(lane_h == 0, 0.0, above) + jnp.where(lane_h == 15, 0.0, below)

    def halo_mid(s):
        return pltpu.roll(s[0:128], 16, 1) + s[128:256] + pltpu.roll(s[256:384], 112, 1)

    sp = halo(w1_ref, xh_ref)
    sg = halo(w2_ref, ch_ref)
    edge[0] = sp[0:128]
    edge[1] = sp[256:384]
    edge[2] = sg[0:128]
    edge[3] = sg[256:384]
    act, slope = gelu_parts(halo_mid(sp))
    hedge[0] = act * maskh_ref[...]
    hedge[1] = halo_mid(sg) * slope * maskh_ref[...]
    for ref in (hs, gps):
        ref[0] = jnp.zeros((384, 256), BF)
        ref[17] = jnp.zeros((384, 256), BF)

    def to_left(tile, row):
        moved = pltpu.roll(tile, 112 - row, 1)
        return jnp.concatenate([moved, moved], axis=1)

    def to_right(tile, row):
        moved = pltpu.roll(tile, 63 - row, 1)
        return jnp.concatenate([moved, moved], axis=1)

    def before(val, tile, row):
        return jnp.where(lane256 == 0, to_left(tile, row), pltpu.roll(val, 1, 1))

    def after(val, tile, row):
        return jnp.where(lane256 == 255, to_right(tile, row), pltpu.roll(val, 255, 1))

    def two_rows(ref, row, height):
        return jnp.concatenate(
            [ref[pl.ds(row, 3)].reshape(3 * height, 256), ref[pl.ds(row + 1, 3)].reshape(3 * height, 256)], axis=1
        )

    def first_stage(q):
        row0 = 2 * q
        zp = dot(w1_ref[...], two_rows(x_ref, row0, 256))
        zg = dot(w2_ref[...], two_rows(c_ref, row0, 256))
        for s in range(2):
            row = row0 + s
            a = zp[:, 256 * s : 256 * s + 256]
            b = zg[:, 256 * s : 256 * s + 256]
            pre = a[128:256] + before(a[0:128], edge[0], row) + after(a[256:384], edge[1], row)
            gh = b[128:256] + before(b[0:128], edge[2], row) + after(b[256:384], edge[3], row)
            mask = mask_ref[row]
            act, slope = gelu_parts(pre)
            for ref, val, tile in ((hs, act * mask, hedge[0]), (gps, gh * slope * mask, hedge[1])):
                ref[row + 1, 0:128] = before(val, tile, row).astype(BF)
                ref[row + 1, 128:256] = val.astype(BF)
                ref[row + 1, 256:384] = after(val, tile, row).astype(BF)

    bufs = ((s1, r1), (s2, r2), (s3, r3))
    order = ((0, 2, 1), (1, 2, 0))

    def hop(step, a, q):
        src, dst = bufs[step]
        return pltpu.make_async_remote_copy(
            src_ref=src.at[a, q], dst_ref=dst.at[a, q], send_sem=send_sem.at[step, a, q], recv_sem=recv_sem.at[step, a, q],
            device_id=partners[order[a][step]], device_id_type=MESH,
        )

    def second_stage(q):
        for a, (w_ref, ref) in enumerate(((w3_ref, hs), (w4_ref, gps))):
            res = dot(w_ref[...], two_rows(ref, 2 * q, 384))
            for s in range(2):
                part = res[:, 256 * s : 256 * s + 256]
                keep[a, q, s] = part[0:128]
                s1[a, q, s] = part[128:256].astype(BF)
            hop(0, a, q).start()

    def advance(step, q):
        left = (64, 32, 0)[step]
        for a in range(2):
            hop(step, a, q).wait_recv()
            for s in range(2):
                got = bufs[step][1][a, q, s].astype(F32)
                if step < 2:
                    total = keep[a, q, s, 0 : 2 * left] + got
                    keep[a, q, s, 0:left] = total[0:left]
                    bufs[step + 1][0][a, q, s] = total[left : 2 * left].astype(BF)
                else:
                    sums_ref[a, 2 * q + s] = keep[a, q, s, 0:32] + got
            if step < 2:
                hop(step + 1, a, q).start()

    def progress(t):
        for step, lag in enumerate((3, 5, 7)):
            @pl.when((t >= lag) & (t < lag + 8))
            def _():
                advance(step, t - lag)

    @pl.loop(0, 9)
    def _(t):
        @pl.when(t < 8)
        def _():
            first_stage(t)

        @pl.when(t == 1)
        def _():
            pl.semaphore_wait(barrier, 11)

        @pl.when(t >= 1)
        def _():
            second_stage(t - 1)

        progress(t)

    def to_mate(g):
        return pltpu.make_async_remote_copy(
            src_ref=gx.at[g], dst_ref=gxr.at[g], send_sem=gxs_sem.at[g], recv_sem=gxr_sem.at[g],
            device_id=mate, device_id_type=MESH,
        )

    def scatter(g, d):
        return pltpu.make_async_remote_copy(
            src_ref=gs.at[g, peer(d)], dst_ref=gr.at[g, d], send_sem=gs_sem.at[g, d], recv_sem=gr_sem.at[g, d],
            device_id=(peer(d) * 2 + core, filt), device_id_type=MESH,
        )

    def spread(g, d):
        return pltpu.make_async_remote_copy(
            src_ref=gall.at[g, chip], dst_ref=gall.at[g, chip], send_sem=ga_sem.at[g, d], recv_sem=gar_sem.at[g, d],
            device_id=(peer(d) * 2 + core, filt), device_id_type=MESH,
        )

    def arrival(g, d):
        return pltpu.make_async_remote_copy(
            src_ref=gall.at[g, chip], dst_ref=gall.at[g, peer(opposite(d))], send_sem=ga_sem.at[g, d], recv_sem=gar_sem.at[g, d],
            device_id=(peer(d) * 2 + core, filt), device_id_type=MESH,
        )

    def across(g):
        return pltpu.make_async_remote_copy(
            src_ref=gall.at[g], dst_ref=goth.at[g], send_sem=go_sem.at[g], recv_sem=gor_sem.at[g],
            device_id=mate, device_id_type=MESH,
        )

    def weight_round(g):
        for a, (ref, other) in enumerate(((hs, c_ref), (gps, x_ref))):
            gacc[a] = jnp.zeros((384, 256), F32)

            @pl.loop(0, 4)
            def _(b):
                left = jnp.concatenate([ref[4 * b + j + g] for j in range(4)], axis=1)
                right = jnp.concatenate([other[4 * b + j + 1] for j in range(4)], axis=1)
                gacc[a] += dot_t(left, right)
        gx[g] = gacc[1 - core].astype(BF)
        to_mate(g).start()

    def gather_mate(g):
        to_mate(g).wait_recv()
        total = gacc[core] + gxr[g].astype(F32)
        total = total.reshape(8, 48, 256)
        gsum[g] = total
        gs[g] = total.astype(BF)
        for d in range(1, 8):
            scatter(g, d).start()

    def finish_piece(g):
        total = gsum[g, chip]
        for d in range(1, 8):
            scatter(g, d).wait_recv()
            total = total + gr[g, d].astype(F32)
        gall[g, chip] = total.astype(BF)
        for d in range(1, 8):
            spread(g, d).start()

    def swap_cores(g):
        for d in range(1, 8):
            arrival(g, d).wait_recv()
        across(g).start()

    @pl.loop(0, 3)
    def _(g):
        weight_round(g)

        @pl.when(g >= 1)
        def _():
            finish_piece(g - 1)

        progress(9 + 2 * g)
        gather_mate(g)
        progress(10 + 2 * g)

        @pl.when(g >= 1)
        def _():
            swap_cores(g - 1)

    finish_piece(2)
    swap_cores(2)
    for g in range(3):
        across(g).wait_recv()
    own = pltpu.make_async_copy(gall, grads_ref.at[core], out_sem.at[0])
    oth = pltpu.make_async_copy(goth, grads_ref.at[1 - core], out_sem.at[1])
    own.start()
    oth.start()

    @pl.loop(0, 8)
    def _(q):
        for step in range(3):
            for a in range(2):
                hop(step, a, q).wait_send()

    @pl.loop(0, 3)
    def _(g):
        to_mate(g).wait_send()
        across(g).wait_send()
        for d in range(1, 8):
            scatter(g, d).wait_send()
            spread(g, d).wait_send()

    own.wait()
    oth.wait()


def call_kernel(*args):
    vm = pltpu.VMEM
    dma = pltpu.SemaphoreType.DMA
    whole = pl.BlockSpec(memory_space=pltpu.VMEM)
    return pl.pallas_call(
        kernel,
        name="ocean_block",
        out_shape=(
            jax.ShapeDtypeStruct((2, 16, 32, 256), F32),
            jax.ShapeDtypeStruct((2, 3, 8, 48, 256), BF),
        ),
        in_specs=[whole] * 10,
        out_specs=(whole, pl.BlockSpec(memory_space=pl.ANY)),
        scratch_shapes=[
            vm((18, 384, 256), BF), vm((18, 384, 256), BF), vm((4, 128, 128), F32), vm((2, 128, 128), F32),
            vm((2, 8, 2, 128, 256), F32),
            vm((2, 8, 2, 128, 256), BF), vm((2, 8, 2, 128, 256), BF),
            vm((2, 8, 2, 64, 256), BF), vm((2, 8, 2, 64, 256), BF),
            vm((2, 8, 2, 32, 256), BF), vm((2, 8, 2, 32, 256), BF),
            vm((2, 384, 256), F32), vm((3, 384, 256), BF), vm((3, 384, 256), BF),
            vm((3, 8, 48, 256), F32), vm((3, 8, 48, 256), BF), vm((3, 8, 48, 256), BF),
            vm((3, 8, 48, 256), BF), vm((3, 8, 48, 256), BF),
            dma((3, 2, 8)), dma((3, 2, 8)), dma((3,)), dma((3,)), dma((3, 8)), dma((3, 8)), dma((3, 8)), dma((3, 8)),
            dma((3,)), dma((3,)), dma((2,)),
        ],
        compiler_params=pltpu.CompilerParams(
            collective_id=1, has_side_effects=True, vmem_limit_bytes=56 * 2**20
        ),
        cost_estimate=pl.CostEstimate(flops=14_500_000_000, bytes_accessed=10_000_000, transcendentals=1_000_000),
    )(*args)


def shards(ocean_state, cotangent, conv_in, conv_out, tile_mask):
    channels, height, breadth = ocean_state.shape
    lon, filt, u, v, y = coords()
    peers = lax.axis_size("lon")
    tiles = tile_mask.shape[1]
    per_dev = breadth // TILE_W
    wide = lax.dynamic_slice_in_dim(
        jnp.concatenate([tile_mask[:, -1:], tile_mask, tile_mask[:, :1]], axis=1), lon * per_dev, per_dev + 2, 1
    ).astype(F32)
    rows = jnp.repeat(wide, TILE_H, axis=0)
    mask = jnp.repeat(rows[:, 1:-1], TILE_W, axis=1)
    maskh = jnp.concatenate(
        [rows[:, 0], rows[:, 0], rows[:, 1], rows[:, -2], rows[:, -1], rows[:, -1], jnp.zeros((32,), F32)]
    )[None, :]

    first = jnp.concatenate([ocean_state[:, :, 0:2], cotangent[:, :, 0:2]], axis=0)
    last = jnp.concatenate([ocean_state[:, :, -2:], cotangent[:, :, -2:]], axis=0)
    first = jnp.swapaxes(first, 1, 2).reshape(2 * channels, 2 * height)
    last = jnp.swapaxes(last, 1, 2).reshape(2 * channels, 2 * height)
    up = [(i, (i + 1) % peers) for i in range(peers)]
    down = [(j, i) for i, j in up]
    left = lax.ppermute(last, "lon", up)
    right = lax.ppermute(first, "lon", down)
    edges = jnp.concatenate(
        [left, first[:, 0:height], last[:, height:], right, jnp.zeros((2 * channels, 32), BF)], axis=1
    ) * maskh.astype(BF)

    mask_bf = mask.astype(BF)

    def by_row(t):
        return jnp.pad(jnp.swapaxes(t * mask_bf, 0, 1), ((1, 1), (0, 0), (0, 0)))

    k_in = conv_in.reshape(3, 3, 256, 128)
    k_out = conv_out.reshape(3, 3, 128, 256)
    w1 = jnp.transpose(k_in, (1, 3, 0, 2)).reshape(384, 768)
    w2 = jnp.transpose(k_out[::-1, ::-1], (1, 2, 0, 3)).reshape(384, 768)
    w3 = jnp.transpose(conv_out, (2, 0, 1)).reshape(8, 32, 1152)
    w4 = jnp.transpose(conv_in[::-1], (1, 0, 2)).reshape(8, 32, 1152)
    w3 = jnp.concatenate(
        [
            lax.dynamic_slice_in_dim(w3, filt_of((u + i) % 2, (v + k) % 2, (y + j) % 2), 1, 0)
            for i in range(2) for j in range(2) for k in range(2)
        ]
    ).reshape(256, 1152)
    w4 = jnp.concatenate(
        [
            lax.dynamic_slice_in_dim(w4, filt_of((u + k) % 2, (v + i) % 2, (y + j) % 2), 1, 0)
            for i in range(2) for j in range(2) for k in range(2)
        ]
    ).reshape(256, 1152)

    sums, grads = call_kernel(
        by_row(ocean_state), by_row(cotangent), edges[:channels], edges[channels:], w1, w2, w3, w4,
        mask[:, None, :], maskh,
    )
    own = channels // lax.axis_size("filt")
    state_own = lax.dynamic_slice_in_dim(ocean_state, filt * own, own, 0)
    cot_own = lax.dynamic_slice_in_dim(cotangent, filt * own, own, 0)
    block_out = (state_own + mask * jnp.swapaxes(sums[0], 0, 1)).astype(BF)
    grad_state = (cot_own + mask * jnp.swapaxes(sums[1], 0, 1)).astype(BF)
    scale = 1.0 / (height * breadth * peers) ** 0.5
    grads = grads.reshape(2, 9, 128, 256)
    grad_out = grads[0].astype(F32) * scale
    grad_in = jnp.swapaxes(grads[1][::-1], 1, 2).astype(F32) * scale
    return (block_out, grad_state, grad_in, grad_out)


def solution(mesh):
    in_specs = (
        P(None, None, "lon"),
        P(None, None, "lon"),
        P(None, None, "filt"),
        P(None, "filt", None),
        P(),
    )
    out_specs = (
        P("filt", None, "lon"),
        P("filt", None, "lon"),
        P(None, None, "filt"),
        P(None, "filt", None),
    )
    return jax.shard_map(shards, mesh=mesh, in_specs=in_specs, out_specs=out_specs, check_vma=False)
```

profile of v0, /device:TPU:1, one launch (start us, length us, event | category | flops | bytes accessed | tf_op | source)
XLA Modules:
  0.0 138.0 jit_solution(10156843202560161639)
XLA Ops:
  0.6 3.1 %fusion.6 = (bf16[256,16,2]{2,1,0:T(8,128)(2,1)S(1)}, bf16[256,16,2]{2,1,0:T(8,128)(2,1)}) fusion(bf16[256,16,256]{2,1,0:T(8,128)(2,1)} %param.5), kind=kLoop, calls=%fused_computation.41 | loop fusion | bytes 65536 | tf_op jit(solution)/shard_map/slice | solution.py:344
  3.8 2.2 %copy.51 = bf16[256,16,2]{0,1,2:T(8,128)(2,1)S(1)} copy(bf16[256,16,2]{2,1,0:T(8,128)(2,1)} %get-tuple-element.21) | data formatting | bytes 32768
  6.0 1.8 %fusion.7 = (bf16[256,16,2]{2,1,0:T(8,128)(2,1)}, bf16[256,16,2]{2,1,0:T(8,128)(2,1)}) fusion(bf16[256,16,256]{2,1,0:T(8,128)(2,1)S(1)} %copy-done), kind=kLoop, calls=%fused_computation.42 | loop fusion | bytes 65536 | tf_op jit(solution)/shard_map/slice | solution.py:344
  7.8 2.2 %copy.52 = bf16[256,16,2]{0,1,2:T(8,128)(2,1)S(1)} copy(bf16[256,16,2]{2,1,0:T(8,128)(2,1)} %get-tuple-element.23) | data formatting | bytes 32768
  10.1 0.1 copy.37
  10.2 3.1 %collective-permute-start = (bf16[512,32]{1,0:T(8,128)(2,1)S(1)}, bf16[512,32]{1,0:T(8,128)(2,1)S(1)}, u32[]{:S(2)}, u32[]{:S(2)}) collective-permute-start(bf16[512,32]{1,0:T(8,128)(2,1)S(1)} %copy.37), channel_id=1, source_target_pairs={{0,8},{8,16},{16,24},{24,32},{32,40},{40,48},{48,56},{56,64},{64,7... | collective-permute-start | bytes 98312 | tf_op jit(solution)/shard_map/ppermute | solution.py:350
  13.3 0.9 copy.53
  14.2 2.2 %copy.54 = bf16[256,16,2]{0,1,2:T(8,128)(2,1)S(1)} copy(bf16[256,16,2]{2,1,0:T(8,128)(2,1)} %get-tuple-element.22) | data formatting | bytes 32768
  16.4 0.1 copy.40
  16.9 1.1 reverse_bitcast_fusion
  18.0 0.4 copy.46
  18.4 1.1 reshape.119
  19.6 1.8 %copy.45 = bf16[256,9,128]{2,1,0:T(8,128)(2,1)S(1)} copy(bf16[256,9,128]{0,2,1:T(8,128)(2,1)} %bitcast.67) | data formatting | bytes 1179648 | tf_op jit(solution)/shard_map/transpose | solution.py:365
  21.4 1.1 reshape.117
  22.6 1.6 %dynamic-slice_dynamic-update-slice_fusion.7 = (bf16[8,32,1152]{2,1,0:T(8,128)(2,1)}, bf16[8,32,1152]{2,1,0:T(8,128)(2,1)S(1)}) fusion(bf16[8,32,1152]{2,1,0:T(8,128)(2,1)} %reshape.119, s32[]{:T(128)S(6)} %select_n.215, bf16[8,32,1152]{2,1,0:T(8,128)(2,1)} %reshape.117), kind=kLoop, calls=%fused_computation.18 | loop fusion | bytes 294916
  24.1 1.5 %dynamic-slice_dynamic-update-slice_fusion.6 = bf16[8,32,1152]{2,1,0:T(8,128)(2,1)} fusion(bf16[8,32,1152]{2,1,0:T(8,128)(2,1)} %get-tuple-element.36, bf16[8,32,1152]{2,1,0:T(8,128)(2,1)} %reshape.119, s32[]{:T(128)S(6)} %select_n.224), kind=kLoop, calls=%fused_computation.17 | loop fusion | bytes 147460
  25.6 1.5 %dynamic-slice_dynamic-update-slice_fusion.5 = bf16[8,32,1152]{2,1,0:T(8,128)(2,1)} fusion(bf16[8,32,1152]{2,1,0:T(8,128)(2,1)} %dynamic-slice_dynamic-update-slice_fusion.6, bf16[8,32,1152]{2,1,0:T(8,128)(2,1)} %reshape.119, s32[]{:T(128)S(6)} %select_n.220), kind=kLoop, calls=%fused_computation.16 | loop fusion | bytes 147460
  27.2 1.5 %dynamic-slice_dynamic-update-slice_fusion.4 = bf16[8,32,1152]{2,1,0:T(8,128)(2,1)} fusion(bf16[8,32,1152]{2,1,0:T(8,128)(2,1)} %dynamic-slice_dynamic-update-slice_fusion.5, bf16[8,32,1152]{2,1,0:T(8,128)(2,1)} %reshape.119, s32[]{:T(128)S(6)} %select_n.227), kind=kLoop, calls=%fused_computation.15 | loop fusion | bytes 147460
  28.7 1.5 %dynamic-slice_dynamic-update-slice_fusion.3 = bf16[8,32,1152]{2,1,0:T(8,128)(2,1)} fusion(bf16[8,32,1152]{2,1,0:T(8,128)(2,1)} %dynamic-slice_dynamic-update-slice_fusion.4, bf16[8,32,1152]{2,1,0:T(8,128)(2,1)} %reshape.119, s32[]{:T(128)S(6)} %select_n.218), kind=kLoop, calls=%fused_computation.14 | loop fusion | bytes 147460
  30.2 0.9 dynamic-slice_dynamic-update-slice_fusion.14
  31.1 0.9 dynamic-slice_dynamic-update-slice_fusion.13
  32.0 1.5 %dynamic-slice_dynamic-update-slice_fusion.2 = bf16[8,32,1152]{2,1,0:T(8,128)(2,1)} fusion(bf16[8,32,1152]{2,1,0:T(8,128)(2,1)} %dynamic-slice_dynamic-update-slice_fusion.3, bf16[8,32,1152]{2,1,0:T(8,128)(2,1)} %reshape.119, s32[]{:T(128)S(6)} %select_n.226), kind=kLoop, calls=%fused_computation.13 | loop fusion | bytes 147460
  33.5 1.5 %dynamic-slice_dynamic-update-slice_fusion.1 = bf16[8,32,1152]{2,1,0:T(8,128)(2,1)} fusion(bf16[8,32,1152]{2,1,0:T(8,128)(2,1)} %dynamic-slice_dynamic-update-slice_fusion.2, bf16[8,32,1152]{2,1,0:T(8,128)(2,1)} %reshape.119, s32[]{:T(128)S(6)} %select_n.221), kind=kLoop, calls=%fused_computation.12 | loop fusion | bytes 147460
  35.1 0.9 dynamic-slice_dynamic-update-slice_fusion.12
  36.0 0.9 dynamic-slice_dynamic-update-slice_fusion.11
  36.9 0.9 dynamic-slice_dynamic-update-slice_fusion.10
  37.7 0.9 dynamic-slice_dynamic-update-slice_fusion.9
  38.6 1.5 %dynamic-slice_dynamic-update-slice_fusion = bf16[8,32,1152]{2,1,0:T(8,128)(2,1)} fusion(bf16[8,32,1152]{2,1,0:T(8,128)(2,1)} %dynamic-slice_dynamic-update-slice_fusion.1, bf16[8,32,1152]{2,1,0:T(8,128)(2,1)} %reshape.119, s32[]{:T(128)S(6)} %select_n.228), kind=kLoop, calls=%fused_computation.11 | loop fusion | bytes 147460 | tf_op jit(solution)/shard_map/concatenate | solution.py:373
  40.2 0.9 dynamic-slice_dynamic-update-slice_fusion.8
  41.3 0.6 copy-done.7
  42.3 6.3 %fusion.4 = (bf16[256,16,256]{2,0,1:T(8,128)(2,1)}, bf16[16,256,256]{2,1,0:T(8,128)(2,1)}, bf16[16,256,256]{2,1,0:T(8,128)(2,1)}, bf16[256,16,256]{2,0,1:T(8,128)(2,1)}) fusion(bf16[256,16,256]{2,1,0:T(8,128)(2,1)S(1)} %copy-done, bf16[16,256]{1,0:T(8,128)(2,1)S(1)} %bitcast.81, bf16[256,16,256]{2,1,0:T(8,128)(2,1)} %param.5), kind=kLoop, calls=%fused_computation.39 | loop fusion | flops 2097152 | bytes 12591104 | tf_op args[1]
  48.8 3.4 %pad.7.x_ref = bf16[18,256,256]{2,1,0:T(8,128)(2,1)} pad(bf16[16,256,256]{2,1,0:T(8,128)(2,1)} %get-tuple-element.34, bf16[]{:T(256)} %constant.209.clone.1), padding=1_1x0_0x0_0 | pad | bytes 4456450 | tf_op jit(solution)/shard_map/jit(_pad)/pad | solution.py:359
  52.2 1.6 %pad.8.c_ref = bf16[18,256,256]{2,1,0:T(8,128)(2,1)} pad(bf16[16,256,256]{2,1,0:T(8,128)(2,1)S(1)} %copy-done.1, bf16[]{:T(256)} %constant.209.clone.1), padding=1_1x0_0x0_0 | pad | bytes 4456450 | tf_op jit(solution)/shard_map/jit(_pad)/pad | solution.py:359
  53.8 0.5 copy.44
  54.3 3.6 %rev.9 = bf16[3,3,128,256]{3,0,2,1:T(4,128)(2,1)S(1)} reverse(bf16[3,3,128,256]{3,0,2,1:T(4,128)(2,1)S(1)} %copy.44), dimensions={0,1} | reverse | bytes 1179648 | tf_op jit(solution)/shard_map/rev | solution.py:364
  57.9 0.9 copy.57
  58.9 0.7 copy.43
  59.6 0.9 copy.56
  60.5 1.2 concatenate.36
  61.7 0.7 fusion.8
  62.4 67.8 %ocean_block.1 = (f32[2,16,32,256]{3,2,1,0:T(8,128)}, bf16[2,3,8,48,256]{4,3,2,1,0:T(8,128)(2,1)}) custom-call(bf16[18,256,256]{2,1,0:T(8,128)(2,1)} %pad.7.x_ref, bf16[18,256,256]{2,1,0:T(8,128)(2,1)} %pad.8.c_ref, bf16[256,128]{1,0:T(8,128)(2,1)} %get-tuple-element.27.xh_ref, bf16[256,128]{1,0:T(8,128)(2,1)} %get-tuple-element.26.ch_ref, ...), custom_call_target="tpu_custom_call" | custom-call | flops 14499999744 | bytes 10000000 | tf_op jit(solution)/shard_map/ocean_block/pallas_call | solution.py:301
  130.2 1.1 slice.78
  131.3 2.3 %convert_multiply_fusion = f32[1,3,8,48,256]{4,3,2,1,0:T(8,128)} fusion(bf16[2,3,8,48,256]{4,3,2,1,0:T(8,128)(2,1)} %get-tuple-element.7), kind=kLoop, calls=%fused_computation.2 | loop fusion | flops 589824 | bytes 1769472 | tf_op jit(solution)/shard_map/mul | solution.py:391
  133.6 0.3 copy.48
  133.9 1.1 multiply_bitcast_fusion.2
  135.0 1.2 fusion
  136.3 0.9 copy.49
  137.1 0.9 copy.50
  (40 shorter events, 1.0 us)
Async XLA Ops:
  0.6 5.4 %copy-start = (bf16[256,16,256]{2,1,0:T(8,128)(2,1)S(1)}, bf16[256,16,256]{2,1,0:T(8,128)(2,1)}, u32[]{:S(2)}) copy-start(bf16[256,16,256]{2,1,0:T(8,128)(2,1)} %param.6) | copy-start | bytes 6291460
  10.2 50.3 %collective-permute-start = (bf16[512,32]{1,0:T(8,128)(2,1)S(1)}, bf16[512,32]{1,0:T(8,128)(2,1)S(1)}, u32[]{:S(2)}, u32[]{:S(2)}) collective-permute-start(bf16[512,32]{1,0:T(8,128)(2,1)S(1)} %copy.37), channel_id=1, source_target_pairs={{0,8},{8,16},{16,24},{24,32},{32,40},{40,48},{48,56},{56,64},{64,7... | collective-permute-start | bytes 98312 | tf_op jit(solution)/shard_map/ppermute | solution.py:350
  16.6 43.9 %collective-permute-start.1 = (bf16[512,32]{1,0:T(8,128)(2,1)S(1)}, bf16[512,32]{1,0:T(8,128)(2,1)}, u32[]{:S(2)}, u32[]{:S(2)}) collective-permute-start(bf16[512,32]{1,0:T(8,128)(2,1)S(1)} %copy.40), channel_id=1, source_target_pairs={{8,0},{16,8},{24,16},{32,24},{40,32},{48,40},{56,48},{64,56},{72,6... | collective-permute-start | bytes 98312 | tf_op jit(solution)/shard_map/ppermute | solution.py:351
  21.4 19.6 %copy-start.6 = (s32[2,32]{1,0:T(2,128)S(1)}, s32[2,32]{1,0:T(2,128)}, u32[]{:S(2)}) copy-start(s32[2,32]{1,0:T(2,128)} %param.9) | copy-start | bytes 772
  41.1 0.8 copy-start.7
  42.3 6.4 %copy-start.5 = (f32[16,2,128]{2,1,0:T(2,128)}, f32[16,2,128]{2,1,0:T(2,128)S(1)}, u32[]{:S(2)}) copy-start(f32[16,2,128]{2,1,0:T(2,128)S(1)} %broadcast_in_dim.18) | copy-start | bytes 49156
  48.8 3.4 %copy-start.8 = (f32[128]{0:T(128)}, f32[128]{0:T(128)S(1)}, u32[]{:S(2)}) copy-start(f32[128]{0:T(128)S(1)} %concatenate.41) | copy-start | bytes 1540
  48.8 3.4 %copy-start.1 = (bf16[16,256,256]{2,1,0:T(8,128)(2,1)S(1)}, bf16[16,256,256]{2,1,0:T(8,128)(2,1)}, u32[]{:S(2)}) copy-start(bf16[16,256,256]{2,1,0:T(8,128)(2,1)} %get-tuple-element.17) | copy-start | bytes 6291460
  52.2 1.6 %copy-start.2 = (bf16[9,128,256]{2,1,0:T(8,128)(2,1)S(1)}, bf16[9,128,256]{2,1,0:T(8,128)(2,1)}, u32[]{:S(2)}) copy-start(bf16[9,128,256]{2,1,0:T(8,128)(2,1)} %param.8) | copy-start | bytes 1769476
  53.8 5.0 %copy-start.3 = (bf16[9,256,128]{2,1,0:T(8,128)(2,1)S(1)}, bf16[9,256,128]{2,1,0:T(8,128)(2,1)}, u32[]{:S(2)}) copy-start(bf16[9,256,128]{2,1,0:T(8,128)(2,1)} %param.7) | copy-start | bytes 1769476
  131.3 3.7 %copy-start.4 = (f32[2,16,32,256]{3,2,1,0:T(8,128)S(1)}, f32[2,16,32,256]{3,2,1,0:T(8,128)}, u32[]{:S(2)}) copy-start(f32[2,16,32,256]{3,2,1,0:T(8,128)} %get-tuple-element.6) | copy-start | bytes 3145732
where the time goes:
time: 139 us; the launch traced here: 138 us
  Pallas kernels  67.8 us (49%)
  local copies, waits for them, and re-layouts  54.8 us (39%)
  other arithmetic  11.1 us (8%)
  starting transfers between devices  3.17 us (2%)
    pallas_call x1, Pallas kernels, call_kernel(): pl.pallas_call(kernel, name='ocean_block', out_shape=(jax.ShapeDtypeStruc...  67.8 us
    unnamed x41, local copies, waits for them, and re-layouts  27.8 us
    unnamed x1, other arithmetic  6.25 us
    pad x2, local copies, waits for them, and re-layouts, by_row(): return jnp.pad(jnp.swapaxes(t * mask_bf, 0, 1), ((1, 1), (0, 0), (0, 0)))  5.03 us
    rev x1, local copies, waits for them, and re-layouts, shards(): w2 = jnp.transpose(k_out[::-1, ::-1], (1, 2, 0, 3)).reshape(384, 768)  3.59 us
    slice x1, local copies, waits for them, and re-layouts, shards(): ocean_state[:, :, 0:2]  3.14 us
    ppermute x1, starting transfers between devices, shards(): left = lax.ppermute(last, 'lon', up)  3.1 us
  transfers between devices with their start and end apart: 2, of which 0 were waited for; matrix products, arithmetic and copies ran while one was open for 33% of the time, Pallas kernels for 0%

commit v1 on v0

v1 whole, which is shorter than its diff:
```python
import functools

import jax
import jax.numpy as jnp
from jax import lax
from jax.experimental import pallas as pl
from jax.experimental.pallas import tpu as pltpu
from jax.sharding import PartitionSpec as P

TILE_H = 8
TILE_W = 128
MESH = pl.DeviceIdType.MESH
BF = jnp.bfloat16
F32 = jnp.float32
ROOT_HALF = 0.7071067811865476
NORM_CONST = 0.3989422804014327


def dot(a, b):
    return lax.dot_general(a, b, (((1,), (0,)), ((), ())), preferred_element_type=F32)


def dot_t(a, b):
    return lax.dot_general(a, b, (((1,), (1,)), ((), ())), preferred_element_type=F32)


def gelu_parts(v):
    e = 0.5 * (1.0 + lax.erf(v * ROOT_HALF))
    return v * e, e + v * jnp.exp(-0.5 * v * v) * NORM_CONST


def coords():
    lon, filt = lax.axis_index("lon"), lax.axis_index("filt")
    y, x = filt // 4, filt % 4
    v = x // 2
    u = (x + v) % 2
    return lon, filt, u, v, y


def filt_of(u, v, y):
    return 4 * y + 2 * v + (u + v) % 2


def kernel(
    x_ref, c_ref, win_ref, wout_ref, tiles_ref,
    block_ref, state_ref, gout_ref, gin_ref,
    xr, cr, w1, w2, w3, w4, maskv, tedge, hal, hs, gps, edge, hedge, keep, s1, r1, s2, r2, s3, r3, sums,
    gacc, gx, gxr, gsum, gs, gr, gall, goth,
    hals_sem, halr_sem, send_sem, recv_sem, gxs_sem, gxr_sem, gs_sem, gr_sem, ga_sem, gar_sem, go_sem, gor_sem,
):
    lon, filt, u, v, y = coords()
    core = lon % 2
    chip = lon // 2
    lane256 = lax.broadcasted_iota(jnp.int32, (128, 256), 1)
    partners = ((lon, filt_of(1 - u, v, y)), (lon, filt_of(u, 1 - v, y)), (lon, filt_of(u, v, 1 - y)))
    mate = (chip * 2 + (1 - core), filt)
    far = ((lon + 15 + 2 * core) % 16, filt)

    def peer(d):
        z, yl = chip % 4, chip // 4
        z = (z + d % 4) % 4
        yl = (yl + d // 4) % 2
        return yl * 4 + z

    def opposite(d):
        return (4 - d % 4) % 4 + (d // 4) * 4

    barrier = pltpu.get_barrier_semaphore()
    for who in partners + (mate, far):
        pl.semaphore_signal(barrier, inc=1, device_id=who, device_id_type=MESH)
    for d in range(1, 8):
        pl.semaphore_signal(barrier, inc=1, device_id=(peer(d) * 2 + core, filt), device_id_type=MESH)

    def flag(tile_row, offset):
        return tiles_ref[tile_row, (2 * lon + 32 + offset) % 32].astype(F32)

    wide = lax.broadcasted_iota(jnp.int32, (1, 256), 1)
    for t in range(2):
        line = jnp.where(wide < 128, flag(t, 0), flag(t, 1))
        for r in range(8):
            maskv[8 * t + r] = line
    laneh = lax.broadcasted_iota(jnp.int32, (1, 128), 1)
    maskh = jnp.where(
        laneh < 64,
        jnp.where(laneh % 8 < 4, flag(0, -1), flag(0, 2)),
        jnp.where(laneh % 8 < 4, flag(1, -1), flag(1, 2)),
    )

    for ref in (xr, cr):
        ref[0] = jnp.zeros((256, 256), BF)
        ref[17] = jnp.zeros((256, 256), BF)
    for ref in (hs, gps):
        ref[0] = jnp.zeros((384, 256), BF)
        ref[17] = jnp.zeros((384, 256), BF)

    @pl.loop(0, 16)
    def _(b):
        part = pl.ds(pl.multiple_of(b * 16, 16), 16)
        m = maskv[...].astype(BF)
        xr[1:17, part, :] = jnp.swapaxes(x_ref[part], 0, 1) * m
        cr[1:17, part, :] = jnp.swapaxes(c_ref[part], 0, 1) * m

    lane_e = lax.broadcasted_iota(jnp.int32, (256, 128), 1)
    for a, ref in enumerate((xr, cr)):
        acc = jnp.zeros((256, 128), F32)
        for r in range(16):
            row = ref[r + 1].astype(F32)
            ends = jnp.where(lane_e < 64, row[:, 0:128], row[:, 128:256])
            acc = jnp.where(lane_e // 8 == r, pltpu.roll(ends, (8 * r + 2) % 128, 1), acc)
        acc = jnp.where(lane_e % 8 < 4, acc, pltpu.roll(acc, 4, 1))
        tedge[a] = acc.astype(BF)

    def halo_copy(i):
        return pltpu.make_async_remote_copy(
            src_ref=tedge, dst_ref=hal.at[i], send_sem=hals_sem.at[i], recv_sem=halr_sem.at[i],
            device_id=(mate, far)[i], device_id_type=MESH,
        )

    pl.semaphore_wait(barrier, 12)
    halo_copy(1).start()
    halo_copy(0).start()

    for k in range(9):
        w2[(k % 3) * 128 : (k % 3) * 128 + 128, (k // 3) * 256 : (k // 3) * 256 + 256] = wout_ref[8 - k]
    eye = (lax.broadcasted_iota(jnp.int32, (128, 128), 0) == lax.broadcasted_iota(jnp.int32, (128, 128), 1))
    flipped = dot_t(eye.astype(F32).astype(BF), win_ref[...].reshape(2304, 128))
    for k in range(9):
        w1[(k % 3) * 128 : (k % 3) * 128 + 128, (k // 3) * 256 : (k // 3) * 256 + 256] = flipped[
            :, k * 256 : k * 256 + 256
        ].astype(BF)
    place = lax.broadcasted_iota(jnp.int32, (256, 256), 0)
    chan = lax.broadcasted_iota(jnp.int32, (256, 256), 1)
    b1, b2, b3, low = place // 128, (place // 64) % 2, (place // 32) % 2, place % 32
    pick_a = (chan == 32 * filt_of((u + b1) % 2, (v + b3) % 2, (y + b2) % 2) + low).astype(F32).astype(BF)
    pick_b = (chan == 32 * filt_of((u + b3) % 2, (v + b1) % 2, (y + b2) % 2) + low).astype(F32).astype(BF)
    w3[...] = dot_t(pick_a, wout_ref[...].reshape(1152, 256)).astype(BF)
    w4[...] = dot(pick_b, jnp.concatenate([win_ref[8 - k] for k in range(9)], axis=1)).astype(BF)

    halo_copy(0).wait_recv()
    halo_copy(1).wait_recv()

    lane_h = lax.broadcasted_iota(jnp.int32, (384, 128), 1)

    def halo(w_ref, a):
        t = jnp.where(
            lane_e % 8 < 2,
            hal[1 - core, a].astype(F32),
            jnp.where(lane_e % 8 >= 6, hal[core, a].astype(F32), tedge[a].astype(F32)),
        ).astype(BF)
        total = dot(w_ref[:, 256:512], t)
        above = pltpu.roll(dot(w_ref[:, 0:256], t), 8, 1)
        below = pltpu.roll(dot(w_ref[:, 512:768], t), 120, 1)
        return total + jnp.where(lane_h < 8, 0.0, above) + jnp.where(lane_h >= 120, 0.0, below)

    def halo_mid(s):
        return pltpu.roll(s[0:128], 1, 1) + s[128:256] + pltpu.roll(s[256:384], 127, 1)

    sp = halo(w1, 0)
    sg = halo(w2, 1)
    edge[0] = sp[0:128]
    edge[1] = sp[256:384]
    edge[2] = sg[0:128]
    edge[3] = sg[256:384]
    act, slope = gelu_parts(halo_mid(sp))
    hedge[0] = act * maskh
    hedge[1] = halo_mid(sg) * slope * maskh

    def before(val, tile, row):
        moved = pltpu.roll(tile, 127 - 8 * row, 1)
        return jnp.where(lane256 == 0, jnp.concatenate([moved, moved], axis=1), pltpu.roll(val, 1, 1))

    def after(val, tile, row):
        moved = pltpu.roll(tile, 121 - 8 * row, 1)
        return jnp.where(lane256 == 255, jnp.concatenate([moved, moved], axis=1), pltpu.roll(val, 255, 1))

    def two_rows(ref, row, height):
        return jnp.concatenate(
            [ref[pl.ds(row, 3)].reshape(3 * height, 256), ref[pl.ds(row + 1, 3)].reshape(3 * height, 256)], axis=1
        )

    def first_stage(q):
        row0 = 2 * q
        zp = dot(w1[...], two_rows(xr, row0, 256))
        zg = dot(w2[...], two_rows(cr, row0, 256))
        for s in range(2):
            row = row0 + s
            a = zp[:, 256 * s : 256 * s + 256]
            b = zg[:, 256 * s : 256 * s + 256]
            pre = a[128:256] + before(a[0:128], edge[0], row) + after(a[256:384], edge[1], row)
            gh = b[128:256] + before(b[0:128], edge[2], row) + after(b[256:384], edge[3], row)
            mask = maskv[row]
            act, slope = gelu_parts(pre)
            for ref, val, tile in ((hs, act * mask, hedge[0]), (gps, gh * slope * mask, hedge[1])):
                ref[row + 1, 0:128] = before(val, tile, row).astype(BF)
                ref[row + 1, 128:256] = val.astype(BF)
                ref[row + 1, 256:384] = after(val, tile, row).astype(BF)

    bufs = ((s1, r1), (s2, r2), (s3, r3))
    order = ((0, 2, 1), (1, 2, 0))

    def hop(step, a, q):
        src, dst = bufs[step]
        return pltpu.make_async_remote_copy(
            src_ref=src.at[a, q], dst_ref=dst.at[a, q], send_sem=send_sem.at[step, a, q], recv_sem=recv_sem.at[step, a, q],
            device_id=partners[order[a][step]], device_id_type=MESH,
        )

    def second_stage(q):
        for a, (w_ref, ref) in enumerate(((w3, hs), (w4, gps))):
            res = dot(w_ref[...], two_rows(ref, 2 * q, 384))
            for s in range(2):
                part = res[:, 256 * s : 256 * s + 256]
                keep[a, q, s] = part[0:128]
                s1[a, q, s] = part[128:256].astype(BF)
            hop(0, a, q).start()

    def advance(step, q):
        left = (64, 32, 0)[step]
        for a in range(2):
            hop(step, a, q).wait_recv()
            for s in range(2):
                got = bufs[step][1][a, q, s].astype(F32)
                if step < 2:
                    total = keep[a, q, s, 0 : 2 * left] + got
                    keep[a, q, s, 0:left] = total[0:left]
                    bufs[step + 1][0][a, q, s] = total[left : 2 * left].astype(BF)
                else:
                    sums[a, 2 * q + s] = keep[a, q, s, 0:32] + got
            if step < 2:
                hop(step + 1, a, q).start()

    def progress(t):
        for step, lag in enumerate((3, 5, 7)):
            @pl.when((t >= lag) & (t < lag + 8))
            def _():
                advance(step, t - lag)

    @pl.loop(0, 9)
    def _(t):
        @pl.when(t < 8)
        def _():
            first_stage(t)

        @pl.when(t >= 1)
        def _():
            second_stage(t - 1)

        progress(t)

    def to_mate(g):
        return pltpu.make_async_remote_copy(
            src_ref=gx.at[g], dst_ref=gxr.at[g], send_sem=gxs_sem.at[g], recv_sem=gxr_sem.at[g],
            device_id=mate, device_id_type=MESH,
        )

    def scatter(g, d):
        return pltpu.make_async_remote_copy(
            src_ref=gs.at[g, peer(d)], dst_ref=gr.at[g, d], send_sem=gs_sem.at[g, d], recv_sem=gr_sem.at[g, d],
            device_id=(peer(d) * 2 + core, filt), device_id_type=MESH,
        )

    def spread(g, d):
        return pltpu.make_async_remote_copy(
            src_ref=gall.at[g, chip], dst_ref=gall.at[g, chip], send_sem=ga_sem.at[g, d], recv_sem=gar_sem.at[g, d],
            device_id=(peer(d) * 2 + core, filt), device_id_type=MESH,
        )

    def arrival(g, d):
        return pltpu.make_async_remote_copy(
            src_ref=gall.at[g, chip], dst_ref=gall.at[g, peer(opposite(d))], send_sem=ga_sem.at[g, d], recv_sem=gar_sem.at[g, d],
            device_id=(peer(d) * 2 + core, filt), device_id_type=MESH,
        )

    def across(g):
        return pltpu.make_async_remote_copy(
            src_ref=gall.at[g], dst_ref=goth.at[g], send_sem=go_sem.at[g], recv_sem=gor_sem.at[g],
            device_id=mate, device_id_type=MESH,
        )

    def four_rows(ref, row):
        return jnp.concatenate([ref[row + j] for j in range(4)], axis=1)

    def weight_round(g):
        gacc[...] = jnp.zeros((2, 6, 128, 128), F32)

        @pl.loop(0, 4)
        def _(b):
            res = dot_t(four_rows(hs, 4 * b + g), four_rows(cr, 4 * b + 1))
            for n in range(6):
                gacc[0, n] += res[(n // 2) * 128 : (n // 2) * 128 + 128, (n % 2) * 128 : (n % 2) * 128 + 128]
            res = dot_t(four_rows(xr, 4 * b + 1), four_rows(gps, 4 * b + g))
            for n in range(6):
                gacc[1, n] += res[(n // 3) * 128 : (n // 3) * 128 + 128, (n % 3) * 128 : (n % 3) * 128 + 128]

        gx[g] = gacc[1 - core].astype(BF)
        to_mate(g).start()

    def gather_mate(g):
        to_mate(g).wait_recv()
        for p in range(8):
            total = gacc[core, :, 16 * p : 16 * p + 16] + gxr[g, :, 16 * p : 16 * p + 16].astype(F32)
            gsum[g, p] = total
            gs[g, p] = total.astype(BF)
        for d in range(1, 8):
            scatter(g, d).start()

    def finish_piece(g):
        total = gsum[g, chip]
        for d in range(1, 8):
            scatter(g, d).wait_recv()
            total = total + gr[g, d].astype(F32)
        gall[g, chip] = total.astype(BF)
        for d in range(1, 8):
            spread(g, d).start()

    def swap_cores(g):
        for d in range(1, 8):
            arrival(g, d).wait_recv()
        across(g).start()

    @pl.loop(0, 3)
    def _(g):
        weight_round(g)

        @pl.when(g >= 1)
        def _():
            finish_piece(g - 1)

        progress(9 + 2 * g)
        gather_mate(g)
        progress(10 + 2 * g)

        @pl.when(g >= 1)
        def _():
            swap_cores(g - 1)

    mine = pl.ds(pl.multiple_of(filt * 32, 32), 32)
    for a, (ref, raw) in enumerate(((block_ref, x_ref), (state_ref, c_ref))):
        ref[...] = (raw[mine].astype(F32) + jnp.swapaxes(sums[a] * maskv[...], 0, 1)).astype(BF)

    finish_piece(2)
    swap_cores(2)
    for g in range(3):
        across(g).wait_recv()

    def put(first, second):
        for g in range(3):
            for p in range(8):
                rows = slice(16 * p, 16 * p + 16)
                for n in range(6):
                    gout_ref[3 * g + n // 2, rows, (n % 2) * 128 : (n % 2) * 128 + 128] = first[g, p, n]
                    half = (n // 3) * 128 + 16 * p
                    gin_ref[8 - (3 * g + n % 3), half : half + 16, :] = second[g, p, n]

    @pl.when(core == 0)
    def _():
        put(gall, goth)

    @pl.when(core == 1)
    def _():
        put(goth, gall)

    halo_copy(0).wait_send()
    halo_copy(1).wait_send()

    @pl.loop(0, 8)
    def _(q):
        for step in range(3):
            for a in range(2):
                hop(step, a, q).wait_send()

    @pl.loop(0, 3)
    def _(g):
        to_mate(g).wait_send()
        across(g).wait_send()
        for d in range(1, 8):
            scatter(g, d).wait_send()
            spread(g, d).wait_send()


def call_kernel(*args):
    vm = pltpu.VMEM
    dma = pltpu.SemaphoreType.DMA
    whole = pl.BlockSpec(memory_space=pltpu.VMEM)
    return pl.pallas_call(
        kernel,
        name="ocean_block",
        out_shape=(
            jax.ShapeDtypeStruct((32, 16, 256), BF),
            jax.ShapeDtypeStruct((32, 16, 256), BF),
            jax.ShapeDtypeStruct((9, 128, 256), BF),
            jax.ShapeDtypeStruct((9, 256, 128), BF),
        ),
        in_specs=[whole] * 4 + [pl.BlockSpec(memory_space=pltpu.SMEM)],
        out_specs=(whole,) * 4,
        scratch_shapes=[
            vm((18, 256, 256), BF), vm((18, 256, 256), BF),
            vm((384, 768), BF), vm((384, 768), BF), vm((256, 1152), BF), vm((256, 1152), BF),
            vm((16, 1, 256), F32), vm((2, 256, 128), BF), vm((2, 2, 256, 128), BF),
            vm((18, 384, 256), BF), vm((18, 384, 256), BF), vm((4, 128, 128), F32), vm((2, 128, 128), F32),
            vm((2, 8, 2, 128, 256), F32),
            vm((2, 8, 2, 128, 256), BF), vm((2, 8, 2, 128, 256), BF),
            vm((2, 8, 2, 64, 256), BF), vm((2, 8, 2, 64, 256), BF),
            vm((2, 8, 2, 32, 256), BF), vm((2, 8, 2, 32, 256), BF),
            vm((2, 16, 32, 256), F32),
            vm((2, 6, 128, 128), F32), vm((3, 6, 128, 128), BF), vm((3, 6, 128, 128), BF),
            vm((3, 8, 6, 16, 128), F32), vm((3, 8, 6, 16, 128), BF), vm((3, 8, 6, 16, 128), BF),
            vm((3, 8, 6, 16, 128), BF), vm((3, 8, 6, 16, 128), BF),
            dma((2,)), dma((2,)),
            dma((3, 2, 8)), dma((3, 2, 8)), dma((3,)), dma((3,)), dma((3, 8)), dma((3, 8)), dma((3, 8)), dma((3, 8)),
            dma((3,)), dma((3,)),
        ],
        compiler_params=pltpu.CompilerParams(
            collective_id=1, has_side_effects=True, vmem_limit_bytes=60 * 2**20
        ),
        cost_estimate=pl.CostEstimate(flops=14_500_000_000, bytes_accessed=10_000_000, transcendentals=1_000_000),
    )(*args)


def shards(ocean_state, cotangent, conv_in, conv_out, tile_mask):
    _, height, breadth = ocean_state.shape
    block_out, grad_state, grad_out, grad_in = call_kernel(ocean_state, cotangent, conv_in, conv_out, tile_mask)
    scale = 1.0 / (height * breadth * lax.axis_size("lon")) ** 0.5
    return (block_out, grad_state, grad_in.astype(F32) * scale, grad_out.astype(F32) * scale)


def solution(mesh):
    in_specs = (
        P(None, None, "lon"),
        P(None, None, "lon"),
        P(None, None, "filt"),
        P(None, "filt", None),
        P(),
    )
    out_specs = (
        P("filt", None, "lon"),
        P("filt", None, "lon"),
        P(None, None, "filt"),
        P(None, "filt", None),
    )
    return jax.shard_map(shards, mesh=mesh, in_specs=in_specs, out_specs=out_specs, check_vma=False)
```

time: 139 us -> 79 us (0.57)
  local copies, waits for them, and re-layouts: 54.8 us -> 1.42 us
  other arithmetic: 11.1 us -> 3.36 us
  Pallas kernels: 67.8 us -> 73.5 us
  starting transfers between devices: 3.17 us -> 0 us
    unnamed x41 -> x8, local copies, waits for them, and re-layouts: 27.8 us -> 1.42 us
    slice x8 -> x0, local copies, waits for them, and re-layouts: 6.98 us -> none  [the longest x1 3.14 us: shards(): ocean_state[:, :, 0:2]]
    unnamed x1 -> x0, other arithmetic: 6.25 us -> none
    pallas_call x1, Pallas kernels: 67.8 us -> 73.5 us  [call_kernel(): pl.pallas_call(kernel, name='ocean_block', out_shape=(jax.ShapeDtypeStruc...]
    pad x2 -> x0, local copies, waits for them, and re-layouts: 5.03 us -> none  [by_row(): return jnp.pad(jnp.swapaxes(t * mask_bf, 0, 1), ((1, 1), (0, 0), (0, 0)))]
    reshape x7 -> x0, local copies, waits for them, and re-layouts: 3.79 us -> none  [the longest x1 1.14 us: shards(): w3 = jnp.transpose(conv_out, (2, 0, 1)).reshape(8, 32, 1152)]
    concatenate x5 -> x0, local copies, waits for them, and re-layouts: 3.67 us -> none  [the longest x1 1.51 us: shards(): jnp.concatenate([lax.dynamic_slice_in_dim(w4, filt_of((u + k) % 2, (v + i...]
    rev x1 -> x0, local copies, waits for them, and re-layouts: 3.59 us -> none  [shards(): w2 = jnp.transpose(k_out[::-1, ::-1], (1, 2, 0, 3)).reshape(384, 768)]
  transfers between devices with their start and end apart: 2 -> 0, of which waited for: 0 -> 0; matrix products, arithmetic and copies ran while one was open for 33% -> 0% of each run, Pallas kernels for 0% -> 0%
where the time goes in v1:
time: 79 us; the launch traced here: 78.9 us
  Pallas kernels  73.5 us (93%)
  other arithmetic  3.36 us (4%)
  local copies, waits for them, and re-layouts  1.42 us (2%)
    pallas_call x1, Pallas kernels, call_kernel(): pl.pallas_call(kernel, name='ocean_block', out_shape=(jax.ShapeDtypeStruc...  73.5 us
    mul x1, other arithmetic, shards(): grad_in.astype(F32) * scale  2.23 us

profile of v1, /device:TPU:1, one launch (start us, length us, event | category | flops | bytes accessed | tf_op | source)
XLA Modules:
  0.0 78.9 jit_solution(12295941368077450016)
XLA Ops:
  0.6 73.5 %ocean_block.1 = (bf16[32,16,256]{2,1,0:T(8,128)(2,1)}, bf16[32,16,256]{2,1,0:T(8,128)(2,1)}, bf16[9,128,256]{2,1,0:T(8,128)(2,1)}, bf16[9,256,128]{2,1,0:T(8,128)(2,1)}) custom-call(bf16[256,16,256]{2,1,0:T(8,128)(2,1)} %x_ref.1, bf16[256,16,256]{2,1,0:T(8,128)(2,1)} %c_ref.1, bf16[9,256,128]{2,1,0:T(8,128)(2,1)} %win_ref.1, bf16[9,128,256]{2,1,0:T(8,128)(2,1)} %wout_ref.1, ...), custom_call_target="tpu_custom_call" | custom-call | flops 14499999744 | bytes 10000000 | tf_op jit(solution)/shard_map/ocean_block/pallas_call | solution.py:385
  74.1 0.0 copy-start
  74.1 2.2 %convert_multiply_fusion.1 = f32[9,256,128]{2,1,0:T(8,128)} fusion(bf16[9,256,128]{2,1,0:T(8,128)(2,1)} %get-tuple-element.10), kind=kLoop, calls=%fused_computation.1 | loop fusion | flops 589824 | bytes 1769472 | tf_op jit(solution)/shard_map/mul | solution.py:424
  76.4 0.0 copy-done
  76.4 0.0 copy-start.2
  76.4 0.0 copy-start.1
  76.4 1.1 %convert_multiply_fusion = f32[9,128,256]{2,1,0:T(8,128)} fusion(bf16[9,128,256]{2,1,0:T(8,128)(2,1)S(1)} %copy-done), kind=kLoop, calls=%fused_computation | loop fusion | flops 589824 | bytes 1769472 | tf_op jit(solution)/shard_map/mul | solution.py:424
  77.5 0.0 copy-done.2
  77.5 0.7 copy.11
  78.2 0.0 copy-done.1
  78.2 0.7 copy.12
Async XLA Ops:
  74.1 2.2 %copy-start = (bf16[9,128,256]{2,1,0:T(8,128)(2,1)S(1)}, bf16[9,128,256]{2,1,0:T(8,128)(2,1)}, u32[]{:S(2)}) copy-start(bf16[9,128,256]{2,1,0:T(8,128)(2,1)} %get-tuple-element.11) | copy-start | bytes 1769476
  76.4 1.1 %copy-start.2 = (bf16[32,16,256]{2,1,0:T(8,128)(2,1)S(1)}, bf16[32,16,256]{2,1,0:T(8,128)(2,1)}, u32[]{:S(2)}) copy-start(bf16[32,16,256]{2,1,0:T(8,128)(2,1)} %get-tuple-element.16) | copy-start | bytes 786436
  76.4 1.8 %copy-start.1 = (bf16[32,16,256]{2,1,0:T(8,128)(2,1)S(1)}, bf16[32,16,256]{2,1,0:T(8,128)(2,1)}, u32[]{:S(2)}) copy-start(bf16[32,16,256]{2,1,0:T(8,128)(2,1)} %get-tuple-element.17) | copy-start | bytes 786436

commit v2 on v1

--- a/solution.py
+++ b/solution.py
@@ -42,11 +42,11 @@
 
 
 def kernel(
-    x_ref, c_ref, win_ref, wout_ref, tiles_ref,
-    block_ref, state_ref, gout_ref, gin_ref,
-    xr, cr, w1, w2, w3, w4, maskv, tedge, hal, hs, gps, edge, hedge, keep, s1, r1, s2, r2, s3, r3, sums,
-    gacc, gx, gxr, gsum, gs, gr, gall, goth,
-    hals_sem, halr_sem, send_sem, recv_sem, gxs_sem, gxr_sem, gs_sem, gr_sem, ga_sem, gar_sem, go_sem, gor_sem,
+    x_hbm, c_hbm, win_hbm, wout_hbm, tiles_ref,
+    block_ref, state_ref, gout_hbm, gin_hbm,
+    x_ref, c_ref, win_ref, wout_ref, gout_ref, gin_ref, xr, cr, w1, w2, w3, w4, maskv, tedge, hal, hs, gps, edge, hedge, keep, s1, r1, s2, r2, s3, r3, sums,
+    gacc, gxr, gsum, gs, gr, gy, gyr, gall, goth,
+    in_sem, win_sem, out_sem, hals_sem, halr_sem, send_sem, recv_sem, gxs_sem, gxr_sem, gs_sem, gr_sem, gys_sem, gyr_sem, ga_sem, gar_sem, go_sem, gor_sem,
 ):
     lon, filt, u, v, y = coords()
     core = lon % 2
@@ -56,20 +56,32 @@
     mate = (chip * 2 + (1 - core), filt)
     far = ((lon + 15 + 2 * core) % 16, filt)
 
-    def peer(d):
-        z, yl = chip % 4, chip // 4
-        z = (z + d % 4) % 4
-        yl = (yl + d // 4) % 2
-        return yl * 4 + z
-
-    def opposite(d):
-        return (4 - d % 4) % 4 + (d // 4) * 4
+    z, yl = chip % 4, chip // 4
+
+    def along(d):
+        return ((yl * 4 + (z + d) % 4) * 2 + core, filt)
+
+    ymate = (((1 - yl) * 4 + z) * 2 + core, filt)
+
+    def take(a, n):
+        part = pl.ds(pl.multiple_of(64 * n, 64), 64)
+        return pltpu.make_async_copy((x_hbm, c_hbm)[a].at[part], (x_ref, c_ref)[a].at[part], in_sem.at[a, n])
+
+    weights_in = (
+        pltpu.make_async_copy(wout_hbm, wout_ref, win_sem.at[0]),
+        pltpu.make_async_copy(win_hbm, win_ref, win_sem.at[1]),
+    )
+    for n in range(4):
+        take(0, n).start()
+        take(1, n).start()
+    for copy in weights_in:
+        copy.start()
 
     barrier = pltpu.get_barrier_semaphore()
-    for who in partners + (mate, far):
+    for who in partners + (mate, far, ymate):
         pl.semaphore_signal(barrier, inc=1, device_id=who, device_id_type=MESH)
-    for d in range(1, 8):
-        pl.semaphore_signal(barrier, inc=1, device_id=(peer(d) * 2 + core, filt), device_id_type=MESH)
+    for d in range(1, 4):
+        pl.semaphore_signal(barrier, inc=1, device_id=along(d), device_id_type=MESH)
 
     def flag(tile_row, offset):
         return tiles_ref[tile_row, (2 * lon + 32 + offset) % 32].astype(F32)
@@ -95,6 +107,11 @@
 
     @pl.loop(0, 16)
     def _(b):
+        @pl.when(b % 4 == 0)
+        def _():
+            take(0, b // 4).wait()
+            take(1, b // 4).wait()
+
         part = pl.ds(pl.multiple_of(b * 16, 16), 16)
         m = maskv[...].astype(BF)
         xr[1:17, part, :] = jnp.swapaxes(x_ref[part], 0, 1) * m
@@ -107,8 +124,7 @@
             row = ref[r + 1].astype(F32)
             ends = jnp.where(lane_e < 64, row[:, 0:128], row[:, 128:256])
             acc = jnp.where(lane_e // 8 == r, pltpu.roll(ends, (8 * r + 2) % 128, 1), acc)
-        acc = jnp.where(lane_e % 8 < 4, acc, pltpu.roll(acc, 4, 1))
-        tedge[a] = acc.astype(BF)
+        tedge[a] = jnp.where(lane_e % 8 < 4, acc, pltpu.roll(acc, 4, 1)).astype(BF)
 
     def halo_copy(i):
         return pltpu.make_async_remote_copy(
@@ -116,10 +132,12 @@
             device_id=(mate, far)[i], device_id_type=MESH,
         )
 
-    pl.semaphore_wait(barrier, 12)
+    pl.semaphore_wait(barrier, 9)
     halo_copy(1).start()
     halo_copy(0).start()
 
+    for copy in weights_in:
+        copy.wait()
     for k in range(9):
         w2[(k % 3) * 128 : (k % 3) * 128 + 128, (k // 3) * 256 : (k // 3) * 256 + 256] = wout_ref[8 - k]
     eye = (lax.broadcasted_iota(jnp.int32, (128, 128), 0) == lax.broadcasted_iota(jnp.int32, (128, 128), 1))
@@ -229,46 +247,34 @@
             if step < 2:
                 hop(step + 1, a, q).start()
 
-    def progress(t):
-        for step, lag in enumerate((3, 5, 7)):
-            @pl.when((t >= lag) & (t < lag + 8))
-            def _():
-                advance(step, t - lag)
-
-    @pl.loop(0, 9)
-    def _(t):
-        @pl.when(t < 8)
-        def _():
-            first_stage(t)
-
-        @pl.when(t >= 1)
-        def _():
-            second_stage(t - 1)
-
-        progress(t)
-
     def to_mate(g):
         return pltpu.make_async_remote_copy(
-            src_ref=gx.at[g], dst_ref=gxr.at[g], send_sem=gxs_sem.at[g], recv_sem=gxr_sem.at[g],
+            src_ref=gacc.at[g, 1 - core], dst_ref=gxr.at[g], send_sem=gxs_sem.at[g], recv_sem=gxr_sem.at[g],
             device_id=mate, device_id_type=MESH,
         )
 
     def scatter(g, d):
         return pltpu.make_async_remote_copy(
-            src_ref=gs.at[g, peer(d)], dst_ref=gr.at[g, d], send_sem=gs_sem.at[g, d], recv_sem=gr_sem.at[g, d],
-            device_id=(peer(d) * 2 + core, filt), device_id_type=MESH,
+            src_ref=gs.at[g, (z + d) % 4], dst_ref=gr.at[g, d], send_sem=gs_sem.at[g, d], recv_sem=gr_sem.at[g, d],
+            device_id=along(d), device_id_type=MESH,
+        )
+
+    def to_ymate(g):
+        return pltpu.make_async_remote_copy(
+            src_ref=gy.at[g], dst_ref=gyr.at[g], send_sem=gys_sem.at[g], recv_sem=gyr_sem.at[g],
+            device_id=ymate, device_id_type=MESH,
         )
 
     def spread(g, d):
         return pltpu.make_async_remote_copy(
-            src_ref=gall.at[g, chip], dst_ref=gall.at[g, chip], send_sem=ga_sem.at[g, d], recv_sem=gar_sem.at[g, d],
-            device_id=(peer(d) * 2 + core, filt), device_id_type=MESH,
+            src_ref=gall.at[g, z], dst_ref=gall.at[g, z], send_sem=ga_sem.at[g, d], recv_sem=gar_sem.at[g, d],
+            device_id=along(d), device_id_type=MESH,
         )
 
     def arrival(g, d):
         return pltpu.make_async_remote_copy(
-            src_ref=gall.at[g, chip], dst_ref=gall.at[g, peer(opposite(d))], send_sem=ga_sem.at[g, d], recv_sem=gar_sem.at[g, d],
-            device_id=(peer(d) * 2 + core, filt), device_id_type=MESH,
+            src_ref=gall.at[g, z], dst_ref=gall.at[g, (z + 4 - d) % 4], send_sem=ga_sem.at[g, d], recv_sem=gar_sem.at[g, d],
+            device_id=along(d), device_id_type=MESH,
         )
 
     def across(g):
@@ -280,85 +286,116 @@
     def four_rows(ref, row):
         return jnp.concatenate([ref[row + j] for j in range(4)], axis=1)
 
-    def weight_round(g):
-        gacc[...] = jnp.zeros((2, 6, 128, 128), F32)
+    def weight_out(g):
+        gacc[g, 0] = jnp.zeros((6, 128, 128), F32)
 
         @pl.loop(0, 4)
         def _(b):
             res = dot_t(four_rows(hs, 4 * b + g), four_rows(cr, 4 * b + 1))
             for n in range(6):
-                gacc[0, n] += res[(n // 2) * 128 : (n // 2) * 128 + 128, (n % 2) * 128 : (n % 2) * 128 + 128]
+                gacc[g, 0, n] += res[(n // 2) * 128 : (n // 2) * 128 + 128, (n % 2) * 128 : (n % 2) * 128 + 128]
+
+    def weight_in(g):
+        gacc[g, 1] = jnp.zeros((6, 128, 128), F32)
+
+        @pl.loop(0, 4)
+        def _(b):
             res = dot_t(four_rows(xr, 4 * b + 1), four_rows(gps, 4 * b + g))
             for n in range(6):
-                gacc[1, n] += res[(n // 3) * 128 : (n // 3) * 128 + 128, (n % 3) * 128 : (n % 3) * 128 + 128]
-
-        gx[g] = gacc[1 - core].astype(BF)
+                gacc[g, 1, n] += res[(n // 3) * 128 : (n // 3) * 128 + 128, (n % 3) * 128 : (n % 3) * 128 + 128]
+
         to_mate(g).start()
 
     def gather_mate(g):
         to_mate(g).wait_recv()
-        for p in range(8):
-            total = gacc[core, :, 16 * p : 16 * p + 16] + gxr[g, :, 16 * p : 16 * p + 16].astype(F32)
+        for p in range(4):
+            rows = slice(32 * p, 32 * p + 32)
+            total = gacc[g, core, :, rows] + gxr[g, :, rows]
             gsum[g, p] = total
             gs[g, p] = total.astype(BF)
-        for d in range(1, 8):
+        for d in range(1, 4):
             scatter(g, d).start()
 
     def finish_piece(g):
-        total = gsum[g, chip]
-        for d in range(1, 8):
+        total = gsum[g, z]
+        for d in range(1, 4):
             scatter(g, d).wait_recv()
             total = total + gr[g, d].astype(F32)
-        gall[g, chip] = total.astype(BF)
-        for d in range(1, 8):
+        gy[g] = total.astype(BF)
+        to_ymate(g).start()
+
+    def finish_both(g):
+        to_ymate(g).wait_recv()
+        gall[g, z] = (gy[g].astype(F32) + gyr[g].astype(F32)).astype(BF)
+        for d in range(1, 4):
             spread(g, d).start()
 
     def swap_cores(g):
-        for d in range(1, 8):
+        for d in range(1, 4):
             arrival(g, d).wait_recv()
         across(g).start()
 
-    @pl.loop(0, 3)
-    def _(g):
-        weight_round(g)
-
-        @pl.when(g >= 1)
+    def put(g):
+        across(g).wait_recv()
+
+        def lay(first, second):
+            @pl.loop(0, 4)
+            def _(p):
+                rows = pl.ds(pl.multiple_of(32 * p, 32), 32)
+                for n in range(6):
+                    gout_ref[3 * g + n // 2, rows, (n % 2) * 128 : (n % 2) * 128 + 128] = first[g, p, n]
+                    half = pl.ds(pl.multiple_of((n // 3) * 128 + 32 * p, 32), 32)
+                    gin_ref[8 - (3 * g + n % 3), half, :] = second[g, p, n]
+
+        @pl.when(core == 0)
         def _():
-            finish_piece(g - 1)
-
-        progress(9 + 2 * g)
-        gather_mate(g)
-        progress(10 + 2 * g)
-
-        @pl.when(g >= 1)
+            lay(gall, goth)
+
+        @pl.when(core == 1)
         def _():
-            swap_cores(g - 1)
+            lay(goth, gall)
+
+        for copy in written(g):
+            copy.start()
+
+    def written(g):
+        return (
+            pltpu.make_async_copy(gout_ref.at[pl.ds(3 * g, 3)], gout_hbm.at[pl.ds(3 * g, 3)], out_sem.at[0, g]),
+            pltpu.make_async_copy(gin_ref.at[pl.ds(6 - 3 * g, 3)], gin_hbm.at[pl.ds(6 - 3 * g, 3)], out_sem.at[1, g]),
+        )
+
+    @pl.loop(0, 13)
+    def _(j):
+        def span(first, count, action):
+            @pl.when((j >= first) & (j < first + count))
+            def _():
+                action(j - first)
+
+        @pl.when(j < 4)
+        def _():
+            @pl.loop(0, 2)
+            def _(i):
+                first_stage(2 * j + i)
+
+        span(0, 8, second_stage)
+        span(4, 3, weight_out)
+        span(5, 3, gather_mate)
+        span(4, 3, weight_in)
+        span(2, 8, functools.partial(advance, 0))
+        span(4, 8, functools.partial(advance, 1))
+        span(5, 8, functools.partial(advance, 2))
+        span(6, 3, finish_piece)
+        span(7, 3, finish_both)
+        span(9, 3, swap_cores)
+        span(10, 2, put)
 
     mine = pl.ds(pl.multiple_of(filt * 32, 32), 32)
     for a, (ref, raw) in enumerate(((block_ref, x_ref), (state_ref, c_ref))):
         ref[...] = (raw[mine].astype(F32) + jnp.swapaxes(sums[a] * maskv[...], 0, 1)).astype(BF)
-
-    finish_piece(2)
-    swap_cores(2)
+    put(2)
     for g in range(3):
-        across(g).wait_recv()
-
-    def put(first, second):
-        for g in range(3):
-            for p in range(8):
-                rows = slice(16 * p, 16 * p + 16)
-                for n in range(6):
-                    gout_ref[3 * g + n // 2, rows, (n % 2) * 128 : (n % 2) * 128 + 128] = first[g, p, n]
-                    half = (n // 3) * 128 + 16 * p
-                    gin_ref[8 - (3 * g + n % 3), half : half + 16, :] = second[g, p, n]
-
-    @pl.when(core == 0)
-    def _():
-        put(gall, goth)
-
-    @pl.when(core == 1)
-    def _():
-        put(goth, gall)
+        for copy in written(g):
+            copy.wait()
 
     halo_copy(0).wait_send()
     halo_copy(1).wait_send()
@@ -373,7 +410,8 @@
     def _(g):
         to_mate(g).wait_send()
         across(g).wait_send()
-        for d in range(1, 8):
+        to_ymate(g).wait_send()
+        for d in range(1, 4):
             scatter(g, d).wait_send()
             spread(g, d).wait_send()
 
@@ -391,9 +429,11 @@
             jax.ShapeDtypeStruct((9, 128, 256), BF),
             jax.ShapeDtypeStruct((9, 256, 128), BF),
         ),
-        in_specs=[whole] * 4 + [pl.BlockSpec(memory_space=pltpu.SMEM)],
-        out_specs=(whole,) * 4,
+        in_specs=[pl.BlockSpec(memory_space=pl.ANY)] * 4 + [pl.BlockSpec(memory_space=pltpu.SMEM)],
+        out_specs=(whole, whole, pl.BlockSpec(memory_space=pl.ANY), pl.BlockSpec(memory_space=pl.ANY)),
         scratch_shapes=[
+            vm((256, 16, 256), BF), vm((256, 16, 256), BF), vm((9, 256, 128), BF), vm((9, 128, 256), BF),
+            vm((9, 128, 256), BF), vm((9, 256, 128), BF),
             vm((18, 256, 256), BF), vm((18, 256, 256), BF),
             vm((384, 768), BF), vm((384, 768), BF), vm((256, 1152), BF), vm((256, 1152), BF),
             vm((16, 1, 256), F32), vm((2, 256, 128), BF), vm((2, 2, 256, 128), BF),
@@ -403,12 +443,13 @@
             vm((2, 8, 2, 64, 256), BF), vm((2, 8, 2, 64, 256), BF),
             vm((2, 8, 2, 32, 256), BF), vm((2, 8, 2, 32, 256), BF),
             vm((2, 16, 32, 256), F32),
-            vm((2, 6, 128, 128), F32), vm((3, 6, 128, 128), BF), vm((3, 6, 128, 128), BF),
-            vm((3, 8, 6, 16, 128), F32), vm((3, 8, 6, 16, 128), BF), vm((3, 8, 6, 16, 128), BF),
-            vm((3, 8, 6, 16, 128), BF), vm((3, 8, 6, 16, 128), BF),
-            dma((2,)), dma((2,)),
-            dma((3, 2, 8)), dma((3, 2, 8)), dma((3,)), dma((3,)), dma((3, 8)), dma((3, 8)), dma((3, 8)), dma((3, 8)),
-            dma((3,)), dma((3,)),
+            vm((3, 2, 6, 128, 128), F32), vm((3, 6, 128, 128), F32),
+            vm((3, 4, 6, 32, 128), F32), vm((3, 4, 6, 32, 128), BF), vm((3, 4, 6, 32, 128), BF),
+            vm((3, 6, 32, 128), BF), vm((3, 6, 32, 128), BF),
+            vm((3, 4, 6, 32, 128), BF), vm((3, 4, 6, 32, 128), BF),
+            dma((2, 4)), dma((2,)), dma((2, 3)), dma((2,)), dma((2,)),
+            dma((3, 2, 8)), dma((3, 2, 8)), dma((3,)), dma((3,)), dma((3, 4)), dma((3, 4)), dma((3,)), dma((3,)),
+            dma((3, 4)), dma((3, 4)), dma((3,)), dma((3,)),
         ],
         compiler_params=pltpu.CompilerParams(
             collective_id=1, has_side_effects=True, vmem_limit_bytes=60 * 2**20
@@ -417,11 +458,58 @@
     )(*args)
 
 
+def finish_kernel(
+    scale, block_in, state_in, gout_in, gin_in, block_out, state_out, gout_out, gin_out, gb, gf, hb, hf, bb, sb, sem,
+):
+    come = tuple(
+        pltpu.make_async_copy(src, dst, sem.at[n])
+        for n, (src, dst) in enumerate(((gout_in, gb), (gin_in, hb), (block_in, bb), (state_in, sb)))
+    )
+    go = tuple(
+        pltpu.make_async_copy(src, dst, sem.at[4 + n])
+        for n, (src, dst) in enumerate(((gf, gout_out), (hf, gin_out), (bb, block_out), (sb, state_out)))
+    )
+    for copy in come:
+        copy.start()
+    for i, (narrow, wide) in enumerate(((gb, gf), (hb, hf))):
+        come[i].wait()
+        wide[...] = narrow[...].astype(F32) * scale
+        go[i].start()
+    for i in (2, 3):
+        come[i].wait()
+        go[i].start()
+    for copy in go:
+        copy.wait()
+
+
+def finish(scale, *args):
+    anywhere = pl.BlockSpec(memory_space=pl.ANY)
+    vm = pltpu.VMEM
+    return pl.pallas_call(
+        functools.partial(finish_kernel, scale),
+        name="widen",
+        out_shape=(
+            jax.ShapeDtypeStruct((32, 16, 256), BF),
+            jax.ShapeDtypeStruct((32, 16, 256), BF),
+            jax.ShapeDtypeStruct((9, 128, 256), F32),
+            jax.ShapeDtypeStruct((9, 256, 128), F32),
+        ),
+        in_specs=[anywhere] * 4,
+        out_specs=(anywhere,) * 4,
+        scratch_shapes=[
+            vm((9, 128, 256), BF), vm((9, 128, 256), F32), vm((9, 256, 128), BF), vm((9, 256, 128), F32),
+            vm((32, 16, 256), BF), vm((32, 16, 256), BF), pltpu.SemaphoreType.DMA((8,)),
+        ],
+        compiler_params=pltpu.CompilerParams(vmem_limit_bytes=62 * 2**20),
+    )(*args)
+
+
 def shards(ocean_state, cotangent, conv_in, conv_out, tile_mask):
     _, height, breadth = ocean_state.shape
-    block_out, grad_state, grad_out, grad_in = call_kernel(ocean_state, cotangent, conv_in, conv_out, tile_mask)
     scale = 1.0 / (height * breadth * lax.axis_size("lon")) ** 0.5
-    return (block_out, grad_state, grad_in.astype(F32) * scale, grad_out.astype(F32) * scale)
+    parts = call_kernel(ocean_state, cotangent, conv_in, conv_out, tile_mask)
+    block_out, grad_state, grad_out, grad_in = finish(scale, *parts)
+    return (block_out, grad_state, grad_in, grad_out)
 
 
 def solution(mesh):

time: 79 us -> 66.9 us (0.85); the launches traced: 78.9 us -> 65.6 us
  Pallas kernels: 73.5 us -> 64.9 us
  other arithmetic: 3.36 us -> 0 us
  local copies, waits for them, and re-layouts: 1.42 us -> 0 us
    pallas_call x1, Pallas kernels: 73.5 us -> 62.2 us  [call_kernel(): pl.pallas_call(kernel, name='ocean_block', out_shape=(jax.ShapeDtypeStruc...]
    mul x2 -> x0, other arithmetic: 3.36 us -> none  [the longest x1 2.23 us: shards(): grad_in.astype(F32) * scale]
    pallas_call x0 -> x1, Pallas kernels: none -> 2.78 us  [finish(): pl.pallas_call(functools.partial(finish_kernel, scale), name='widen', out...]
    unnamed x8 -> x0, local copies, waits for them, and re-layouts: 1.42 us -> none
where the time goes in v2:
time: 66.9 us; the launch traced here: 65.6 us
  Pallas kernels  64.9 us (97%)
    pallas_call x1, Pallas kernels, call_kernel(): pl.pallas_call(kernel, name='ocean_block', out_shape=(jax.ShapeDtypeStruc...  62.2 us
    pallas_call x1, Pallas kernels, finish(): pl.pallas_call(functools.partial(finish_kernel, scale), name='widen', out...  2.78 us

profile of v2, /device:TPU:1, one launch (start us, length us, event | category | flops | bytes accessed | tf_op | source)
XLA Modules:
  0.0 65.6 jit_solution(7739604475324735853)
XLA Ops:
  0.6 62.2 %ocean_block.1 = (bf16[32,16,256]{2,1,0:T(8,128)(2,1)}, bf16[32,16,256]{2,1,0:T(8,128)(2,1)}, bf16[9,128,256]{2,1,0:T(8,128)(2,1)}, bf16[9,256,128]{2,1,0:T(8,128)(2,1)}) custom-call(bf16[256,16,256]{2,1,0:T(8,128)(2,1)} %x_hbm.1, bf16[256,16,256]{2,1,0:T(8,128)(2,1)} %c_hbm.1, bf16[9,256,128]{2,1,0:T(8,128)(2,1)} %win_hbm.1, bf16[9,128,256]{2,1,0:T(8,128)(2,1)} %wout_hbm.1, ...), custom_call_target="tpu_custom_call" | custom-call | flops 14499999744 | bytes 10000000 | tf_op jit(solution)/shard_map/ocean_block/pallas_call | solution.py:423
  62.8 2.8 %widen.1 = (bf16[32,16,256]{2,1,0:T(8,128)(2,1)}, bf16[32,16,256]{2,1,0:T(8,128)(2,1)}, f32[9,128,256]{2,1,0:T(8,128)}, f32[9,256,128]{2,1,0:T(8,128)}) custom-call(bf16[32,16,256]{2,1,0:T(8,128)(2,1)} %get-tuple-element.12.block_in, bf16[32,16,256]{2,1,0:T(8,128)(2,1)} %get-tuple-element.13.state_in, bf16[9,128,256]{2,1,0:T(8,128)(2,1)} %get-tuple-element.14.gout_in, ...), custom_call_target="tpu_custom_call" | custom-call | tf_op jit(solution)/shard_map/widen/pallas_call | solution.py:488

commit v3 on v2

--- a/solution.py
+++ b/solution.py
@@ -44,7 +44,7 @@
 def kernel(
     x_hbm, c_hbm, win_hbm, wout_hbm, tiles_ref,
     block_ref, state_ref, gout_hbm, gin_hbm,
-    x_ref, c_ref, win_ref, wout_ref, gout_ref, gin_ref, xr, cr, w1, w2, w3, w4, maskv, tedge, hal, hs, gps, edge, hedge, keep, s1, r1, s2, r2, s3, r3, sums,
+    x_ref, c_ref, win_ref, wout_ref, gout_ref, gin_ref, xr, cr, w1, w2, w3, w4, maskv, choose, tacc, tedge, hal, hs, gps, edge, hedge, keep, s1, r1, s2, r2, s3, r3, sums,
     gacc, gxr, gsum, gs, gr, gy, gyr, gall, goth,
     in_sem, win_sem, out_sem, hals_sem, halr_sem, send_sem, recv_sem, gxs_sem, gxr_sem, gs_sem, gr_sem, gys_sem, gyr_sem, ga_sem, gar_sem, go_sem, gor_sem,
 ):
@@ -105,6 +105,16 @@
         ref[0] = jnp.zeros((384, 256), BF)
         ref[17] = jnp.zeros((384, 256), BF)
 
+    spot = lax.broadcasted_iota(jnp.int32, (512, 128), 0)
+    slot = lax.broadcasted_iota(jnp.int32, (512, 128), 1)
+
+    @pl.loop(0, 4)
+    def _(g):
+        hit = (slot // 8 == 4 * g + spot // 128) & ((slot % 4 + 126) % 128 == spot % 128)
+        choose[g] = hit.astype(F32).astype(BF)
+
+    tacc[...] = jnp.zeros((2, 256, 128), F32)
+
     @pl.loop(0, 16)
     def _(b):
         @pl.when(b % 4 == 0)
@@ -118,13 +128,17 @@
         cr[1:17, part, :] = jnp.swapaxes(c_ref[part], 0, 1) * m
 
     lane_e = lax.broadcasted_iota(jnp.int32, (256, 128), 1)
-    for a, ref in enumerate((xr, cr)):
-        acc = jnp.zeros((256, 128), F32)
-        for r in range(16):
-            row = ref[r + 1].astype(F32)
-            ends = jnp.where(lane_e < 64, row[:, 0:128], row[:, 128:256])
-            acc = jnp.where(lane_e // 8 == r, pltpu.roll(ends, (8 * r + 2) % 128, 1), acc)
-        tedge[a] = jnp.where(lane_e % 8 < 4, acc, pltpu.roll(acc, 4, 1)).astype(BF)
+
+    @pl.loop(0, 4)
+    def _(g):
+        for a, ref in enumerate((xr, cr)):
+            ends = []
+            for r in range(4):
+                row = ref[4 * g + r + 1]
+                ends.append(jnp.where(lane_e < 64, row[:, 0:128], row[:, 128:256]))
+            tacc[a] += dot(jnp.concatenate(ends, axis=1), choose[g])
+
+    tedge[...] = tacc[...].astype(BF)
 
     def halo_copy(i):
         return pltpu.make_async_remote_copy(
@@ -149,7 +163,7 @@
     place = lax.broadcasted_iota(jnp.int32, (256, 256), 0)
     chan = lax.broadcasted_iota(jnp.int32, (256, 256), 1)
     b1, b2, b3, low = place // 128, (place // 64) % 2, (place // 32) % 2, place % 32
-    pick_a = (chan == 32 * filt_of((u + b1) % 2, (v + b3) % 2, (y + b2) % 2) + low).astype(F32).astype(BF)
+    pick_a = (chan == 32 * filt_of((u + b1) % 2, (v + b2) % 2, (y + b3) % 2) + low).astype(F32).astype(BF)
     pick_b = (chan == 32 * filt_of((u + b3) % 2, (v + b1) % 2, (y + b2) % 2) + low).astype(F32).astype(BF)
     w3[...] = dot_t(pick_a, wout_ref[...].reshape(1152, 256)).astype(BF)
     w4[...] = dot(pick_b, jnp.concatenate([win_ref[8 - k] for k in range(9)], axis=1)).astype(BF)
@@ -214,7 +228,7 @@
                 ref[row + 1, 256:384] = after(val, tile, row).astype(BF)
 
     bufs = ((s1, r1), (s2, r2), (s3, r3))
-    order = ((0, 2, 1), (1, 2, 0))
+    order = ((0, 1, 2), (1, 2, 0))
 
     def hop(step, a, q):
         src, dst = bufs[step]
@@ -436,7 +450,7 @@
             vm((9, 128, 256), BF), vm((9, 256, 128), BF),
             vm((18, 256, 256), BF), vm((18, 256, 256), BF),
             vm((384, 768), BF), vm((384, 768), BF), vm((256, 1152), BF), vm((256, 1152), BF),
-            vm((16, 1, 256), F32), vm((2, 256, 128), BF), vm((2, 2, 256, 128), BF),
+            vm((16, 1, 256), F32), vm((4, 512, 128), BF), vm((2, 256, 128), F32), vm((2, 256, 128), BF), vm((2, 2, 256, 128), BF),
             vm((18, 384, 256), BF), vm((18, 384, 256), BF), vm((4, 128, 128), F32), vm((2, 128, 128), F32),
             vm((2, 8, 2, 128, 256), F32),
             vm((2, 8, 2, 128, 256), BF), vm((2, 8, 2, 128, 256), BF),
@@ -461,21 +475,26 @@
 def finish_kernel(
     scale, block_in, state_in, gout_in, gin_in, block_out, state_out, gout_out, gin_out, gb, gf, hb, hf, bb, sb, sem,
 ):
-    come = tuple(
-        pltpu.make_async_copy(src, dst, sem.at[n])
-        for n, (src, dst) in enumerate(((gout_in, gb), (gin_in, hb), (block_in, bb), (state_in, sb)))
-    )
-    go = tuple(
-        pltpu.make_async_copy(src, dst, sem.at[4 + n])
-        for n, (src, dst) in enumerate(((gf, gout_out), (hf, gin_out), (bb, block_out), (sb, state_out)))
-    )
+    pieces = [(gout_in, gb, gf, gout_out, n) for n in range(3)] + [(gin_in, hb, hf, gin_out, n) for n in range(3)]
+    thirds = [pl.ds(3 * n, 3) for n in range(3)]
+    come = [
+        pltpu.make_async_copy(src.at[thirds[n]], narrow.at[thirds[n]], sem.at[0, i])
+        for i, (src, narrow, _, _, n) in enumerate(pieces)
+    ]
+    go = [
+        pltpu.make_async_copy(wide.at[thirds[n]], dst.at[thirds[n]], sem.at[1, i])
+        for i, (_, _, wide, dst, n) in enumerate(pieces)
+    ]
+    for i, (src, held, dst) in enumerate(((block_in, bb, block_out), (state_in, sb, state_out))):
+        come.append(pltpu.make_async_copy(src, held, sem.at[0, 6 + i]))
+        go.append(pltpu.make_async_copy(held, dst, sem.at[1, 6 + i]))
     for copy in come:
         copy.start()
-    for i, (narrow, wide) in enumerate(((gb, gf), (hb, hf))):
+    for i, (_, narrow, wide, _, n) in enumerate(pieces):
         come[i].wait()
-        wide[...] = narrow[...].astype(F32) * scale
+        wide[thirds[n]] = narrow[thirds[n]].astype(F32) * scale
         go[i].start()
-    for i in (2, 3):
+    for i in (6, 7):
         come[i].wait()
         go[i].start()
     for copy in go:
@@ -498,7 +517,7 @@
         out_specs=(anywhere,) * 4,
         scratch_shapes=[
             vm((9, 128, 256), BF), vm((9, 128, 256), F32), vm((9, 256, 128), BF), vm((9, 256, 128), F32),
-            vm((32, 16, 256), BF), vm((32, 16, 256), BF), pltpu.SemaphoreType.DMA((8,)),
+            vm((32, 16, 256), BF), vm((32, 16, 256), BF), pltpu.SemaphoreType.DMA((2, 8)),
         ],
         compiler_params=pltpu.CompilerParams(vmem_limit_bytes=62 * 2**20),
     )(*args)

time: 66.9 us -> 65.8 us (0.984); the launches traced: 65.6 us -> 65.6 us
  no operation moved by 1% of the time
where the time goes in v3:
time: 65.8 us; the launch traced here: 65.6 us
  Pallas kernels  65 us (99%)
    pallas_call x1, Pallas kernels, call_kernel(): pl.pallas_call(kernel, name='ocean_block', out_shape=(jax.ShapeDtypeStruc...  62.3 us
    pallas_call x1, Pallas kernels, finish(): pl.pallas_call(functools.partial(finish_kernel, scale), name='widen', out...  2.66 us

profile of v3, /device:TPU:1, one launch (start us, length us, event | category | flops | bytes accessed | tf_op | source)
XLA Modules:
  0.0 65.6 jit_solution(10042273439986269561)
XLA Ops:
  0.6 62.3 %ocean_block.1 = (bf16[32,16,256]{2,1,0:T(8,128)(2,1)}, bf16[32,16,256]{2,1,0:T(8,128)(2,1)}, bf16[9,128,256]{2,1,0:T(8,128)(2,1)}, bf16[9,256,128]{2,1,0:T(8,128)(2,1)}) custom-call(bf16[256,16,256]{2,1,0:T(8,128)(2,1)} %x_hbm.1, bf16[256,16,256]{2,1,0:T(8,128)(2,1)} %c_hbm.1, bf16[9,256,128]{2,1,0:T(8,128)(2,1)} %win_hbm.1, bf16[9,128,256]{2,1,0:T(8,128)(2,1)} %wout_hbm.1, ...), custom_call_target="tpu_custom_call" | custom-call | flops 14499999744 | bytes 10000000 | tf_op jit(solution)/shard_map/ocean_block/pallas_call | solution.py:437
  63.0 2.7 %widen.1 = (bf16[32,16,256]{2,1,0:T(8,128)(2,1)}, bf16[32,16,256]{2,1,0:T(8,128)(2,1)}, f32[9,128,256]{2,1,0:T(8,128)}, f32[9,256,128]{2,1,0:T(8,128)}) custom-call(bf16[32,16,256]{2,1,0:T(8,128)(2,1)} %get-tuple-element.12.block_in, bf16[32,16,256]{2,1,0:T(8,128)(2,1)} %get-tuple-element.13.state_in, bf16[9,128,256]{2,1,0:T(8,128)(2,1)} %get-tuple-element.14.gout_in, ...), custom_call_target="tpu_custom_call" | custom-call | tf_op jit(solution)/shard_map/widen/pallas_call | solution.py:507

commit v4 on v3

--- a/solution.py
+++ b/solution.py
@@ -300,23 +300,16 @@
     def four_rows(ref, row):
         return jnp.concatenate([ref[row + j] for j in range(4)], axis=1)
 
-    def weight_out(g):
-        gacc[g, 0] = jnp.zeros((6, 128, 128), F32)
+    def weight_round(g):
+        gacc[g] = jnp.zeros((2, 6, 128, 128), F32)
 
         @pl.loop(0, 4)
         def _(b):
             res = dot_t(four_rows(hs, 4 * b + g), four_rows(cr, 4 * b + 1))
+            other = dot_t(four_rows(xr, 4 * b + 1), four_rows(gps, 4 * b + g))
             for n in range(6):
                 gacc[g, 0, n] += res[(n // 2) * 128 : (n // 2) * 128 + 128, (n % 2) * 128 : (n % 2) * 128 + 128]
-
-    def weight_in(g):
-        gacc[g, 1] = jnp.zeros((6, 128, 128), F32)
-
-        @pl.loop(0, 4)
-        def _(b):
-            res = dot_t(four_rows(xr, 4 * b + 1), four_rows(gps, 4 * b + g))
-            for n in range(6):
-                gacc[g, 1, n] += res[(n // 3) * 128 : (n // 3) * 128 + 128, (n % 3) * 128 : (n % 3) * 128 + 128]
+                gacc[g, 1, n] += other[(n // 3) * 128 : (n // 3) * 128 + 128, (n % 3) * 128 : (n % 3) * 128 + 128]
 
         to_mate(g).start()
 
@@ -392,9 +385,8 @@
                 first_stage(2 * j + i)
 
         span(0, 8, second_stage)
-        span(4, 3, weight_out)
+        span(4, 3, weight_round)
         span(5, 3, gather_mate)
-        span(4, 3, weight_in)
         span(2, 8, functools.partial(advance, 0))
         span(4, 8, functools.partial(advance, 1))
         span(5, 8, functools.partial(advance, 2))

time: 65.8 us -> 65.8 us (level)
  no operation moved by 1% of the time
where the time goes in v4:
time: 65.8 us; the launch traced here: 65.6 us
  Pallas kernels  65 us (99%)
    pallas_call x1, Pallas kernels, call_kernel(): pl.pallas_call(kernel, name='ocean_block', out_shape=(jax.ShapeDtypeStruc...  62.3 us
    pallas_call x1, Pallas kernels, finish(): pl.pallas_call(functools.partial(finish_kernel, scale), name='widen', out...  2.66 us

profile of v4, /device:TPU:1, one launch (start us, length us, event | category | flops | bytes accessed | tf_op | source)
XLA Modules:
  0.0 65.6 jit_solution(2647596866099321805)
XLA Ops:
  0.6 62.3 %ocean_block.1 = (bf16[32,16,256]{2,1,0:T(8,128)(2,1)}, bf16[32,16,256]{2,1,0:T(8,128)(2,1)}, bf16[9,128,256]{2,1,0:T(8,128)(2,1)}, bf16[9,256,128]{2,1,0:T(8,128)(2,1)}) custom-call(bf16[256,16,256]{2,1,0:T(8,128)(2,1)} %x_hbm.1, bf16[256,16,256]{2,1,0:T(8,128)(2,1)} %c_hbm.1, bf16[9,256,128]{2,1,0:T(8,128)(2,1)} %win_hbm.1, bf16[9,128,256]{2,1,0:T(8,128)(2,1)} %wout_hbm.1, ...), custom_call_target="tpu_custom_call" | custom-call | flops 14499999744 | bytes 10000000 | tf_op jit(solution)/shard_map/ocean_block/pallas_call | solution.py:429
  63.0 2.7 %widen.1 = (bf16[32,16,256]{2,1,0:T(8,128)(2,1)}, bf16[32,16,256]{2,1,0:T(8,128)(2,1)}, f32[9,128,256]{2,1,0:T(8,128)}, f32[9,256,128]{2,1,0:T(8,128)}) custom-call(bf16[32,16,256]{2,1,0:T(8,128)(2,1)} %get-tuple-element.12.block_in, bf16[32,16,256]{2,1,0:T(8,128)(2,1)} %get-tuple-element.13.state_in, bf16[9,128,256]{2,1,0:T(8,128)(2,1)} %get-tuple-element.14.gout_in, ...), custom_call_target="tpu_custom_call" | custom-call | tf_op jit(solution)/shard_map/widen/pallas_call | solution.py:499

commit v5 on v3

--- a/solution.py
+++ b/solution.py
@@ -393,9 +393,9 @@
 
         span(0, 8, second_stage)
         span(4, 3, weight_out)
+        span(2, 8, functools.partial(advance, 0))
         span(5, 3, gather_mate)
         span(4, 3, weight_in)
-        span(2, 8, functools.partial(advance, 0))
         span(4, 8, functools.partial(advance, 1))
         span(5, 8, functools.partial(advance, 2))
         span(6, 3, finish_piece)

time: 65.8 us -> 65.8 us (level)
  no operation moved by 1% of the time
where the time goes in v5:
time: 65.8 us; the launch traced here: 65.6 us
  Pallas kernels  65 us (99%)
    pallas_call x1, Pallas kernels, call_kernel(): pl.pallas_call(kernel, name='ocean_block', out_shape=(jax.ShapeDtypeStruc...  62.3 us
    pallas_call x1, Pallas kernels, finish(): pl.pallas_call(functools.partial(finish_kernel, scale), name='widen', out...  2.66 us

profile of v5, /device:TPU:1, one launch (start us, length us, event | category | flops | bytes accessed | tf_op | source)
XLA Modules:
  0.0 65.6 jit_solution(8154831540676417312)
XLA Ops:
  0.6 62.3 %ocean_block.1 = (bf16[32,16,256]{2,1,0:T(8,128)(2,1)}, bf16[32,16,256]{2,1,0:T(8,128)(2,1)}, bf16[9,128,256]{2,1,0:T(8,128)(2,1)}, bf16[9,256,128]{2,1,0:T(8,128)(2,1)}) custom-call(bf16[256,16,256]{2,1,0:T(8,128)(2,1)} %x_hbm.1, bf16[256,16,256]{2,1,0:T(8,128)(2,1)} %c_hbm.1, bf16[9,256,128]{2,1,0:T(8,128)(2,1)} %win_hbm.1, bf16[9,128,256]{2,1,0:T(8,128)(2,1)} %wout_hbm.1, ...), custom_call_target="tpu_custom_call" | custom-call | flops 14499999744 | bytes 10000000 | tf_op jit(solution)/shard_map/ocean_block/pallas_call | solution.py:437
  63.0 2.7 %widen.1 = (bf16[32,16,256]{2,1,0:T(8,128)(2,1)}, bf16[32,16,256]{2,1,0:T(8,128)(2,1)}, f32[9,128,256]{2,1,0:T(8,128)}, f32[9,256,128]{2,1,0:T(8,128)}) custom-call(bf16[32,16,256]{2,1,0:T(8,128)(2,1)} %get-tuple-element.12.block_in, bf16[32,16,256]{2,1,0:T(8,128)(2,1)} %get-tuple-element.13.state_in, bf16[9,128,256]{2,1,0:T(8,128)(2,1)} %get-tuple-element.14.gout_in, ...), custom_call_target="tpu_custom_call" | custom-call | tf_op jit(solution)/shard_map/widen/pallas_call | solution.py:507
